TPU v7x, 32 devices: a whole 2x2x4 slice. The times are simulated.
32 devices in a mesh: bulk: 8 (over z, x), slab: 4 (over y, core).
Axes of the slice: x: 2, y: 2, z: 4, core: 2. Of those that a mesh axis runs over, the one named last changes fastest.
Arguments:
- pressure: float32 [128, 256, 128], P('bulk', 'slab'), may hold values from -12 to 12
- rhs: float32 [128, 256, 128], P('bulk', 'slab'), may hold values from -48 to 48
- kappa: float32 [128, 256, 128], P('bulk', 'slab'), may hold values from 0.5 to 8
- owner: int32 [4, 8, 1024, 1], P('slab', 'bulk'), may hold values from 0 to 7; in each aligned block of 1024 rows (0 to 1023, 1024 to 2047, ..., all dimensions but the last counted through in order) at most 320 rows name the same one
- coarse_row: int32 [4, 8, 1024], P('slab', 'bulk'), may hold values from 0 to 127
- coarse_leak: float32 [4, 1024, 128], P('slab', 'bulk'), may hold values from 1 to 16
- coarse_link: float32 [4, 1024, 128], P('slab', 'bulk'), may hold values from 1 to 16
Outputs:
- pressure_out: float32 [128, 256, 128], P('bulk', 'slab')
Inputs may be any that keep to these rules, and one draw needn't show every extreme that they name: Among the 1024 fine rows of one device, at most 320 name the same owner; in every draw some device gives exactly 320 rows to some owner.
All inputs are finite; a program needn't handle non-finite values.
Results may differ from a plain program's by a relative error of at most 0.00002.
Values sent between devices are 32-bit elements; how exact they have to be, the bound alone decides.
A program may use at most 64 MiB of HBM per device.

v0:
```python
import jax
import jax.numpy as jnp
from jax import lax
from jax.sharding import PartitionSpec as P

SWEEPS = 2
COARSE_SWEEPS = 3


damping = 0.8


def extended_2(block, sides, width):
    for axis, dim in sides:
        count = lax.axis_size(axis)
        forward = [(i, i + 1) for i in range(count - 1)]
        backward = [(target, source) for source, target in forward]
        low = lax.ppermute(
            lax.slice_in_dim(block, block.shape[dim] - width, None, axis=dim), axis, forward
        )
        high = lax.ppermute(lax.slice_in_dim(block, 0, width, axis=dim), axis, backward)
        block = jnp.concatenate([low, block, high], axis=dim)
    return block


def shift_up(values):
    return jnp.concatenate([values[..., 1:], jnp.zeros_like(values[..., :1])], axis=-1)


def shift_down(values):
    return jnp.concatenate([jnp.zeros_like(values[..., :1]), values[..., :-1]], axis=-1)


def face_set(kappa, kappa_rims):
    west_face = 0.5 * (kappa + kappa_rims[:-2, 1:-1])
    east_face = 0.5 * (kappa + kappa_rims[2:, 1:-1])
    south_face = 0.5 * (kappa + kappa_rims[1:-1, :-2])
    north_face = 0.5 * (kappa + kappa_rims[1:-1, 2:])
    lower_face = 0.5 * (kappa + shift_down(kappa))
    upper_face = 0.5 * (kappa + shift_up(kappa))
    faces = (west_face, east_face, south_face, north_face, lower_face, upper_face)
    diagonal = west_face + east_face + south_face + north_face + lower_face + upper_face
    return (faces, diagonal)


def operate(field, faces):
    field_rims = extended_2(field, (("bulk", 0), ("slab", 1)), 1)
    west_face, east_face, south_face, north_face, lower_face, upper_face = faces
    result = west_face * (field - field_rims[:-2, 1:-1]) + east_face * (
        field - field_rims[2:, 1:-1]
    )
    result = (
        result
        + south_face * (field - field_rims[1:-1, :-2])
        + north_face * (field - field_rims[1:-1, 2:])
    )
    result = (
        result + lower_face * (field - shift_down(field)) + upper_face * (field - shift_up(field))
    )
    return result


def coarse_smooth(coarse_rhs, leak, link):
    link_below = shift_down(link)
    cdiag = leak + link + link_below
    correction = jnp.zeros_like(coarse_rhs)
    for sweep_index in range(COARSE_SWEEPS):
        applied = (
            leak * correction
            + link * (correction - shift_up(correction))
            + link_below * (correction - shift_down(correction))
        )
        correction = correction + damping * (coarse_rhs - applied) / cdiag
    return correction


def per_device(pressure, rhs, kappa, owner, coarse_row, coarse_leak, coarse_link):
    kappa_rims = extended_2(kappa, (("bulk", 0), ("slab", 1)), 1)
    faces, diagonal = face_set(kappa, kappa_rims)
    field = pressure
    for sweep_index in range(SWEEPS):
        field = field + damping * (rhs - operate(field, faces)) / diagonal
    residual = rhs - operate(field, faces)
    cells_x, cells_y, depth_cells = residual.shape
    row_total = cells_x * cells_y
    residual_rows = residual.reshape(row_total, depth_cells)
    owners = owner.reshape(row_total)
    targets = coarse_row.reshape(row_total)
    leak = coarse_leak[0]
    link = coarse_link[0]
    coarse_count = leak.shape[0]
    bulk_count = lax.axis_size("bulk")
    capacity = max(2, row_total * 5 // (2 * bulk_count))
    onehot = (owners[:, None] == jnp.arange(bulk_count, dtype=jnp.int32)[None, :]).astype(jnp.int32)
    before = jnp.cumsum(onehot, axis=0) - onehot
    slot_index = jnp.sum(before * onehot, axis=1)
    slot_place = owners * capacity + slot_index
    outgoing = (
        jnp.zeros((bulk_count * capacity, depth_cells), jnp.float32)
        .at[slot_place]
        .set(residual_rows)
    )
    labels = jnp.full((bulk_count * capacity,), coarse_count, jnp.int32).at[slot_place].set(targets)
    arrived, arrived_labels = (
        lax.all_to_all(
            outgoing.reshape(bulk_count, capacity, depth_cells),
            "bulk",
            split_axis=0,
            concat_axis=0,
            tiled=True,
        ),
        lax.all_to_all(
            labels.reshape(bulk_count, capacity), "bulk", split_axis=0, concat_axis=0, tiled=True
        ),
    )
    flat_labels = arrived_labels.reshape(-1)
    coarse_rhs = jax.ops.segment_sum(
        arrived.reshape(-1, depth_cells), flat_labels, num_segments=coarse_count
    )
    correction = coarse_smooth(coarse_rhs, leak, link)
    extended = jnp.concatenate([correction, jnp.zeros((1, depth_cells), jnp.float32)], axis=0)
    replies = extended[flat_labels].reshape(bulk_count, capacity, depth_cells)
    returned = lax.all_to_all(replies, "bulk", split_axis=0, concat_axis=0, tiled=True)
    fine_correction = returned.reshape(bulk_count * capacity, depth_cells)[slot_place]
    field = field + fine_correction.reshape(cells_x, cells_y, depth_cells)
    for sweep_index in range(SWEEPS):
        field = field + damping * (rhs - operate(field, faces)) / diagonal
    return field


def solution(mesh):
    return jax.shard_map(
        per_device,
        mesh=mesh,
        in_specs=(
            P("bulk", "slab", None),
            P("bulk", "slab", None),
            P("bulk", "slab", None),
            P("slab", "bulk", None, None),
            P("slab", "bulk", None),
            P("slab", "bulk", None),
            P("slab", "bulk", None),
        ),
        out_specs=P("bulk", "slab", None),
        check_vma=False,
    )
```

profile of v0, /device:TPU:0, one launch (start us, length us, event | category | flops | bytes accessed | tf_op | source)
XLA Modules:
  0.0 216.1 jit_solution(3652637990638294446)
XLA Ops:
  0.0 0.8 fusion.129
  0.8 4.8 %collective-permute-start = (f32[1,64,128]{2,1,0:T(8,128)S(1)}, f32[1,64,128]{2,1,0:T(8,128)S(1)}, u32[]{:S(2)}, u32[]{:S(2)}) collective-permute-start(f32[1,64,128]{2,1,0:T(8,128)S(1)} %get-tuple-element.41), channel_id=1, source_target_pairs={{0,4},{4,8},{8,12},{12,16},{16,20},{20,24},{24,28},{1,5},{5,9},{9,... | collective-permute-start | bytes 98312 | tf_op jit(solution)/shard_map/ppermute | solution.py:18
  5.6 1.3 collective-permute-start.2
  6.9 0.8 fusion.131
  7.7 4.5 %collective-permute-start.1 = (f32[1,64,128]{2,1,0:T(8,128)S(1)}, f32[1,64,128]{2,1,0:T(8,128)S(1)}, u32[]{:S(2)}, u32[]{:S(2)}) collective-permute-start(f32[1,64,128]{2,1,0:T(8,128)S(1)} %get-tuple-element.45), channel_id=1, source_target_pairs={{0,4},{4,8},{8,12},{12,16},{16,20},{20,24},{24,28},{1,5},{5,9},{9,... | collective-permute-start | bytes 98312 | tf_op jit(solution)/shard_map/ppermute | solution.py:18
  12.3 1.4 collective-permute-start.3
  13.7 3.2 %fusion.128 = (f32[16,64,127]{2,1,0:T(8,128)S(1)}, f32[16,64,127]{2,1,0:T(8,128)}, f32[16,64,127]{2,1,0:T(8,128)}, f32[16,64,127]{2,1,0:T(8,128)}) fusion(f32[16,64,128]{2,1,0:T(8,128)} %param.9, f32[16,64,128]{2,1,0:T(8,128)} %param.7), kind=kLoop, calls=%fused_computation.206 | loop fusion | bytes 4161536 | tf_op jit(solution)/shard_map/slice | solution.py:27
  16.9 2.3 %reduce-window.6 = s32[8,8,128]{2,1,0:T(8,128)S(1)} reduce-window(s32[8,8,128]{2,1,0:T(8,128)S(1)} %fusion.112, s32[]{:T(128)} %constant.13.clone.1), window={size=1x1x128 pad=0_0x0_0x127_0}, to_apply=%region_0.0 | reduce-window | flops 1040384 | bytes 65540 | tf_op jit(solution)/shard_map/reduce-window
  19.2 0.3 slice_reduce_fusion
  19.7 1.3 collective-permute-start.4
  21.0 1.3 collective-permute-start.6
  22.4 4.8 %collective-permute-start.5 = (f32[18,1,128]{2,1,0:T(1,128)S(1)}, f32[18,1,128]{2,1,0:T(1,128)S(1)}, u32[]{:S(2)}, u32[]{:S(2)}) collective-permute-start(f32[18,1,128]{2,1,0:T(1,128)S(1)} %get-tuple-element.20), channel_id=1, source_target_pairs={{0,1},{1,2},{2,3},{4,5},{5,6},{6,7},{8,9},{9,10},{10,11},{12,13},{... | collective-permute-start | bytes 27656 | tf_op jit(solution)/shard_map/ppermute | solution.py:18
  27.2 1.3 collective-permute-start.7
  28.6 2.9 %collective-permute-done.7 = f32[18,1,128]{2,1,0:T(1,128)S(1)} collective-permute-done((f32[18,1,128]{2,1,0:T(1,128)S(1)}, f32[18,1,128]{2,1,0:T(1,128)S(1)}, u32[]{:S(2)}, u32[]{:S(2)}) %collective-permute-start.7) | collective-permute-done | bytes 9248 | tf_op jit(solution)/shard_map/ppermute | solution.py:21
  31.6 2.3 %fusion.75 = (f32[16,64,128]{2,1,0:T(8,128)S(1)}, f32[16,64,128]{2,1,0:T(8,128)S(1)}, f32[16,64,128]{2,1,0:T(8,128)S(1)}, f32[16,64,128]{2,1,0:T(8,128)S(1)}, f32[16,64,128]{2,1,0:T(8,128)S(1)}) fusion(f32[16,64,128]{2,1,0:T(8,128)S(1)} %copy-done.10, f32[16,64,128]{2,1,0:T(8,128)S(1)} %copy-done.1, f32[18,1,128]{2,1,0:T(1,128)S(1)} %collective-permute-done.7, ...), kind=kLoop, calls=%fused_computation.113 | loop fusion | flops 6029312 | bytes 7622656 | tf_op jit(solution)/shard_map/add | solution.py:82
  33.9 5.0 %collective-permute-start.8 = (f32[1,64,128]{2,1,0:T(8,128)S(1)}, f32[1,64,128]{2,1,0:T(8,128)S(1)}, u32[]{:S(2)}, u32[]{:S(2)}) collective-permute-start(f32[1,64,128]{2,1,0:T(8,128)S(1)} %get-tuple-element.36), channel_id=1, source_target_pairs={{0,4},{4,8},{8,12},{12,16},{16,20},{20,24},{24,28},{1,5},{5,9},{9,... | collective-permute-start | bytes 98312 | tf_op jit(solution)/shard_map/ppermute | solution.py:18
  38.9 1.3 collective-permute-start.9
  40.3 0.3 collective-permute-done.8
  40.5 5.1 %collective-permute-done.9 = f32[1,64,128]{2,1,0:T(8,128)S(1)} collective-permute-done((f32[1,64,128]{2,1,0:T(8,128)S(1)}, f32[1,64,128]{2,1,0:T(8,128)S(1)}, u32[]{:S(2)}, u32[]{:S(2)}) %collective-permute-start.9) | collective-permute-done | bytes 32800 | tf_op jit(solution)/shard_map/ppermute | solution.py:21
  45.7 3.2 %collective-permute-start.10 = (f32[18,1,128]{2,1,0:T(1,128)S(1)}, f32[18,1,128]{2,1,0:T(1,128)S(1)}, u32[]{:S(2)}, u32[]{:S(2)}) collective-permute-start(f32[18,1,128]{2,1,0:T(1,128)S(1)} %get-tuple-element.16), channel_id=1, source_target_pairs={{0,1},{1,2},{2,3},{4,5},{5,6},{6,7},{8,9},{9,10},{10,11},{12,13},{... | collective-permute-start | bytes 27656 | tf_op jit(solution)/shard_map/ppermute | solution.py:18
  48.8 1.3 collective-permute-start.11
  50.4 2.2 %collective-permute-done.11 = f32[18,1,128]{2,1,0:T(1,128)S(1)} collective-permute-done((f32[18,1,128]{2,1,0:T(1,128)S(1)}, f32[18,1,128]{2,1,0:T(1,128)S(1)}, u32[]{:S(2)}, u32[]{:S(2)}) %collective-permute-start.11) | collective-permute-done | bytes 9248 | tf_op jit(solution)/shard_map/ppermute | solution.py:21
  52.6 0.7 fusion.58
  53.3 4.8 %collective-permute-start.12 = (f32[1,64,128]{2,1,0:T(8,128)S(1)}, f32[1,64,128]{2,1,0:T(8,128)S(1)}, u32[]{:S(2)}, u32[]{:S(2)}) collective-permute-start(f32[1,64,128]{2,1,0:T(8,128)S(1)} %get-tuple-element.32), channel_id=1, source_target_pairs={{0,4},{4,8},{8,12},{12,16},{16,20},{20,24},{24,28},{1,5},{5,9},{9,... | collective-permute-start | bytes 98312 | tf_op jit(solution)/shard_map/ppermute | solution.py:18
  58.2 1.3 collective-permute-start.13
  59.5 4.5 %scatter_custom_fusion = s32[2560]{0:T(1024)S(1)} fusion(s32[1024]{0:T(1024)S(1)} %bitcast.86, s32[1024]{0:T(1024)} %bitcast.90, s32[]{:T(128)} %constant.11.clone.1), kind=kCustom, calls=%fused_computation.192 | custom fusion | bytes 10752 | tf_op jit(solution)/shard_map/scatter | solution.py:103
  64.0 0.7 all_to_all.12
  64.6 5.9 %all-to-all-start = ((s32[8,1,320]{2,1,0:T(1,128)}), s32[8,1,320]{2,1,0:T(1,128)S(1)}, u32[]{:S(2)}, u32[]{:S(2)}) async-start(s32[8,1,320]{2,1,0:T(1,128)} %all_to_all.12), calls=%async_computation | async-start | bytes 24576 | tf_op jit(solution)/shard_map/all_to_all | solution.py:112
  70.7 3.6 %collective-permute-start.14 = (f32[18,1,128]{2,1,0:T(1,128)S(1)}, f32[18,1,128]{2,1,0:T(1,128)S(1)}, u32[]{:S(2)}, u32[]{:S(2)}) collective-permute-start(f32[18,1,128]{2,1,0:T(1,128)S(1)} %get-tuple-element.14), channel_id=1, source_target_pairs={{0,1},{1,2},{2,3},{4,5},{5,6},{6,7},{8,9},{9,10},{10,11},{12,13},{... | collective-permute-start | bytes 27656 | tf_op jit(solution)/shard_map/ppermute | solution.py:18
  74.3 1.3 collective-permute-start.15
  75.6 0.2 fusion.124
  75.8 1.9 collective-permute-done.15
  77.7 0.6 fusion.41
  78.4 4.2 %scatter_custom_fusion.1 = f32[2560,128]{1,0:T(8,128)} fusion(s32[1024]{0:T(1024)S(1)} %bitcast.87, f32[1024,128]{1,0:T(8,128)S(1)} %bitcast.82, f32[]{:T(128)} %constant.9.clone.1), kind=kCustom, calls=%fused_computation.5 | custom fusion | bytes 1310724 | tf_op jit(solution)/shard_map/scatter | solution.py:101
  82.6 0.6 copy-done.14
  83.2 6.0 %all-to-all-start.1 = ((f32[8,320,128]{2,1,0:T(8,128)}), f32[8,320,128]{2,1,0:T(8,128)S(1)}, u32[]{:S(2)}, u32[]{:S(2)}) async-start(f32[8,320,128]{2,1,0:T(8,128)} %bitcast.8), calls=%async_computation.1 | async-start | bytes 2621440 | tf_op jit(solution)/shard_map/all_to_all | solution.py:105
  89.2 0.7 reduce.1
  89.9 0.7 reshape.144
  90.6 0.7 broadcast_in_dim_reshape.4
  91.2 0.7 fusion.113
  92.0 29.3 %all-to-all-done.1 = f32[8,320,128]{2,1,0:T(8,128)S(1)} async-done(((f32[8,320,128]{2,1,0:T(8,128)}), f32[8,320,128]{2,1,0:T(8,128)S(1)}, u32[]{:S(2)}, u32[]{:S(2)}) %all-to-all-start.1) | async-done | bytes 1310752 | tf_op jit(solution)/shard_map/all_to_all | solution.py:105
  121.3 14.9 %scatter_custom_fusion.2 = f32[128,128]{1,0:T(8,128)} fusion(s32[2560]{0:T(1024)} %reshape.144, f32[2560,128]{1,0:T(8,128)S(1)} %bitcast.81, f32[]{:T(128)} %constant.9.clone.1), kind=kCustom, calls=%fused_computation.168 | custom fusion | flops 327680 | bytes 66048 | tf_op jit(solution)/shard_map/scatter-add | solution.py:117
  136.2 1.0 fusion.106
  137.2 1.0 fusion.104
  138.5 5.6 %gather_fusion = f32[2560,128]{1,0:T(8,128)} fusion(f32[129,128]{1,0:T(8,128)S(1)} %concatenate.183, s32[3072]{0:T(1024)S(1)} %pad_clamp_fusion), kind=kCustom, calls=%fused_computation | custom fusion | bytes 2631680 | tf_op jit(solution)/shard_map/gather | solution.py:122
  144.1 4.2 %all-to-all-start.2 = ((f32[8,320,128]{2,1,0:T(8,128)}), f32[8,320,128]{2,1,0:T(8,128)S(1)}, u32[]{:S(2)}, u32[]{:S(2)}) async-start(f32[8,320,128]{2,1,0:T(8,128)} %bitcast.76), calls=%async_computation.2 | async-start | bytes 2621440 | tf_op jit(solution)/shard_map/all_to_all | solution.py:123
  148.3 32.1 %all-to-all-done.2 = f32[8,320,128]{2,1,0:T(8,128)S(1)} async-done(((f32[8,320,128]{2,1,0:T(8,128)}), f32[8,320,128]{2,1,0:T(8,128)S(1)}, u32[]{:S(2)}, u32[]{:S(2)}) %all-to-all-start.2) | async-done | bytes 1310752 | tf_op jit(solution)/shard_map/all_to_all | solution.py:123
  180.4 4.0 %gather_fusion.1 = f32[1024,128]{1,0:T(8,128)} fusion(f32[2560,128]{1,0:T(8,128)S(1)} %bitcast.75, s32[1024]{0:T(1024)S(1)} %broadcast_clamp_fusion), kind=kCustom, calls=%fused_computation.1 | custom fusion | bytes 1052672 | tf_op jit(solution)/shard_map/gather | solution.py:124
  184.4 1.1 add.268
  185.5 3.4 %collective-permute-start.16 = (f32[1,64,128]{2,1,0:T(8,128)S(1)}, f32[1,64,128]{2,1,0:T(8,128)S(1)}, u32[]{:S(2)}, u32[]{:S(2)}) collective-permute-start(f32[1,64,128]{2,1,0:T(8,128)S(1)} %get-tuple-element.28), channel_id=1, source_target_pairs={{0,4},{4,8},{8,12},{12,16},{16,20},{20,24},{24,28},{1,5},{5,9},{9,... | collective-permute-start | bytes 98312 | tf_op jit(solution)/shard_map/ppermute | solution.py:18
  188.9 1.4 collective-permute-start.17
  190.4 4.4 %collective-permute-done.17 = f32[1,64,128]{2,1,0:T(8,128)S(1)} collective-permute-done((f32[1,64,128]{2,1,0:T(8,128)S(1)}, f32[1,64,128]{2,1,0:T(8,128)S(1)}, u32[]{:S(2)}, u32[]{:S(2)}) %collective-permute-start.17) | collective-permute-done | bytes 32800 | tf_op jit(solution)/shard_map/ppermute | solution.py:21
  194.9 1.3 collective-permute-start.18
  196.2 1.3 collective-permute-start.19
  197.7 1.5 collective-permute-done.19
  199.2 0.7 fusion.27
  199.9 2.8 %collective-permute-start.20 = (f32[1,64,128]{2,1,0:T(8,128)S(1)}, f32[1,64,128]{2,1,0:T(8,128)S(1)}, u32[]{:S(2)}, u32[]{:S(2)}) collective-permute-start(f32[1,64,128]{2,1,0:T(8,128)S(1)} %get-tuple-element.24), channel_id=1, source_target_pairs={{0,4},{4,8},{8,12},{12,16},{16,20},{20,24},{24,28},{1,5},{5,9},{9,... | collective-permute-start | bytes 98312 | tf_op jit(solution)/shard_map/ppermute | solution.py:18
  202.8 1.3 collective-permute-start.21
  204.1 0.3 collective-permute-done.20
  204.3 4.3 %collective-permute-done.21 = f32[1,64,128]{2,1,0:T(8,128)S(1)} collective-permute-done((f32[1,64,128]{2,1,0:T(8,128)S(1)}, f32[1,64,128]{2,1,0:T(8,128)S(1)}, u32[]{:S(2)}, u32[]{:S(2)}) %collective-permute-start.21) | collective-permute-done | bytes 32800 | tf_op jit(solution)/shard_map/ppermute | solution.py:21
  208.7 2.0 collective-permute-start.22
  210.7 1.3 collective-permute-start.23
  212.2 2.4 %collective-permute-done.23 = f32[18,1,128]{2,1,0:T(1,128)S(1)} collective-permute-done((f32[18,1,128]{2,1,0:T(1,128)S(1)}, f32[18,1,128]{2,1,0:T(1,128)S(1)}, u32[]{:S(2)}, u32[]{:S(2)}) %collective-permute-start.23) | collective-permute-done | bytes 9248 | tf_op jit(solution)/shard_map/ppermute | solution.py:21
  214.6 1.5 fusion.10
  (76 shorter events, 1.6 us)
Async XLA Ops:
  0.8 18.8 %collective-permute-start = (f32[1,64,128]{2,1,0:T(8,128)S(1)}, f32[1,64,128]{2,1,0:T(8,128)S(1)}, u32[]{:S(2)}, u32[]{:S(2)}) collective-permute-start(f32[1,64,128]{2,1,0:T(8,128)S(1)} %get-tuple-element.41), channel_id=1, source_target_pairs={{0,4},{4,8},{8,12},{12,16},{16,20},{20,24},{24,28},{1,5},{5,9},{9,... | collective-permute-start | bytes 98312 | tf_op jit(solution)/shard_map/ppermute | solution.py:18
  5.6 14.1 %collective-permute-start.2 = (f32[1,64,128]{2,1,0:T(8,128)S(1)}, f32[1,64,128]{2,1,0:T(8,128)S(1)}, u32[]{:S(2)}, u32[]{:S(2)}) collective-permute-start(f32[1,64,128]{2,1,0:T(8,128)S(1)} %get-tuple-element.40), channel_id=1, source_target_pairs={{4,0},{8,4},{12,8},{16,12},{20,16},{24,20},{28,24},{5,1},{9,5},{13... | collective-permute-start | bytes 98312 | tf_op jit(solution)/shard_map/ppermute | solution.py:21
  7.7 14.6 %collective-permute-start.1 = (f32[1,64,128]{2,1,0:T(8,128)S(1)}, f32[1,64,128]{2,1,0:T(8,128)S(1)}, u32[]{:S(2)}, u32[]{:S(2)}) collective-permute-start(f32[1,64,128]{2,1,0:T(8,128)S(1)} %get-tuple-element.45), channel_id=1, source_target_pairs={{0,4},{4,8},{8,12},{12,16},{16,20},{20,24},{24,28},{1,5},{5,9},{9,... | collective-permute-start | bytes 98312 | tf_op jit(solution)/shard_map/ppermute | solution.py:18
  12.2 4.6 %copy-start.15 = (s32[1,1,1024,1]{2,3,1,0:T(1,128)S(1)}, s32[1,1,1024,1]{2,3,1,0:T(1,128)}, u32[]{:S(2)}) copy-start(s32[1,1,1024,1]{2,3,1,0:T(1,128)} %param.10) | copy-start | bytes 12292
  12.3 7.4 %copy-start = (f32[16,64,128]{2,1,0:T(8,128)S(1)}, f32[16,64,128]{2,1,0:T(8,128)}, u32[]{:S(2)}) copy-start(f32[16,64,128]{2,1,0:T(8,128)} %param.9) | copy-start | bytes 1572868
  12.3 10.1 %collective-permute-start.3 = (f32[1,64,128]{2,1,0:T(8,128)S(1)}, f32[1,64,128]{2,1,0:T(8,128)S(1)}, u32[]{:S(2)}, u32[]{:S(2)}) collective-permute-start(f32[1,64,128]{2,1,0:T(8,128)S(1)} %get-tuple-element.44), channel_id=1, source_target_pairs={{4,0},{8,4},{12,8},{16,12},{20,16},{24,20},{28,24},{5,1},{9,5},{13... | collective-permute-start | bytes 98312 | tf_op jit(solution)/shard_map/ppermute | solution.py:21
  16.9 5.5 %copy-start.10 = (f32[16,64,128]{2,1,0:T(8,128)S(1)}, f32[16,64,128]{2,1,0:T(8,128)}, u32[]{:S(2)}) copy-start(f32[16,64,128]{2,1,0:T(8,128)} %param.7) | copy-start | bytes 1572868
  16.9 14.7 %copy-start.1 = (f32[16,64,128]{2,1,0:T(8,128)S(1)}, f32[16,64,128]{2,1,0:T(8,128)}, u32[]{:S(2)}) copy-start(f32[16,64,128]{2,1,0:T(8,128)} %param.8) | copy-start | bytes 1572868
  19.7 8.9 %collective-permute-start.4 = (f32[18,1,128]{2,1,0:T(1,128)S(1)}, f32[18,1,128]{2,1,0:T(1,128)S(1)}, u32[]{:S(2)}, u32[]{:S(2)}) collective-permute-start(f32[18,1,128]{2,1,0:T(1,128)S(1)} %get-tuple-element.19), channel_id=1, source_target_pairs={{0,1},{1,2},{2,3},{4,5},{5,6},{6,7},{8,9},{9,10},{10,11},{12,13},{... | collective-permute-start | bytes 27656 | tf_op jit(solution)/shard_map/ppermute | solution.py:18
  21.0 7.6 %collective-permute-start.6 = (f32[18,1,128]{2,1,0:T(1,128)S(1)}, f32[18,1,128]{2,1,0:T(1,128)S(1)}, u32[]{:S(2)}, u32[]{:S(2)}) collective-permute-start(f32[18,1,128]{2,1,0:T(1,128)S(1)} %get-tuple-element.18), channel_id=1, source_target_pairs={{1,0},{2,1},{3,2},{5,4},{6,5},{7,6},{9,8},{10,9},{11,10},{13,12},{... | collective-permute-start | bytes 27656 | tf_op jit(solution)/shard_map/ppermute | solution.py:21
  22.4 6.2 %collective-permute-start.5 = (f32[18,1,128]{2,1,0:T(1,128)S(1)}, f32[18,1,128]{2,1,0:T(1,128)S(1)}, u32[]{:S(2)}, u32[]{:S(2)}) collective-permute-start(f32[18,1,128]{2,1,0:T(1,128)S(1)} %get-tuple-element.20), channel_id=1, source_target_pairs={{0,1},{1,2},{2,3},{4,5},{5,6},{6,7},{8,9},{9,10},{10,11},{12,13},{... | collective-permute-start | bytes 27656 | tf_op jit(solution)/shard_map/ppermute | solution.py:18
  27.2 4.3 %collective-permute-start.7 = (f32[18,1,128]{2,1,0:T(1,128)S(1)}, f32[18,1,128]{2,1,0:T(1,128)S(1)}, u32[]{:S(2)}, u32[]{:S(2)}) collective-permute-start(f32[18,1,128]{2,1,0:T(1,128)S(1)} %get-tuple-element.21), channel_id=1, source_target_pairs={{1,0},{2,1},{3,2},{5,4},{6,5},{7,6},{9,8},{10,9},{11,10},{13,12},{... | collective-permute-start | bytes 27656 | tf_op jit(solution)/shard_map/ppermute | solution.py:21
  33.9 18.7 %copy-start.4 = (f32[16,64,128]{2,1,0:T(8,128)}, f32[16,64,128]{2,1,0:T(8,128)S(1)}, u32[]{:S(2)}) copy-start(f32[16,64,128]{2,1,0:T(8,128)S(1)} %get-tuple-element.8) | copy-start | bytes 1572868
  33.9 18.7 %copy-start.7 = (f32[16,64,128]{2,1,0:T(8,128)}, f32[16,64,128]{2,1,0:T(8,128)S(1)}, u32[]{:S(2)}) copy-start(f32[16,64,128]{2,1,0:T(8,128)S(1)} %get-tuple-element.9) | copy-start | bytes 1572868
  33.9 43.8 %copy-start.2 = (f32[16,64,128]{2,1,0:T(8,128)}, f32[16,64,128]{2,1,0:T(8,128)S(1)}, u32[]{:S(2)}) copy-start(f32[16,64,128]{2,1,0:T(8,128)S(1)} %get-tuple-element.7) | copy-start | bytes 1572868
  33.9 6.6 %collective-permute-start.8 = (f32[1,64,128]{2,1,0:T(8,128)S(1)}, f32[1,64,128]{2,1,0:T(8,128)S(1)}, u32[]{:S(2)}, u32[]{:S(2)}) collective-permute-start(f32[1,64,128]{2,1,0:T(8,128)S(1)} %get-tuple-element.36), channel_id=1, source_target_pairs={{0,4},{4,8},{8,12},{12,16},{16,20},{20,24},{24,28},{1,5},{5,9},{9,... | collective-permute-start | bytes 98312 | tf_op jit(solution)/shard_map/ppermute | solution.py:18
  38.9 6.7 %collective-permute-start.9 = (f32[1,64,128]{2,1,0:T(8,128)S(1)}, f32[1,64,128]{2,1,0:T(8,128)S(1)}, u32[]{:S(2)}, u32[]{:S(2)}) collective-permute-start(f32[1,64,128]{2,1,0:T(8,128)S(1)} %get-tuple-element.37), channel_id=1, source_target_pairs={{4,0},{8,4},{12,8},{16,12},{20,16},{24,20},{28,24},{5,1},{9,5},{13... | collective-permute-start | bytes 98312 | tf_op jit(solution)/shard_map/ppermute | solution.py:21
  45.7 4.7 %collective-permute-start.10 = (f32[18,1,128]{2,1,0:T(1,128)S(1)}, f32[18,1,128]{2,1,0:T(1,128)S(1)}, u32[]{:S(2)}, u32[]{:S(2)}) collective-permute-start(f32[18,1,128]{2,1,0:T(1,128)S(1)} %get-tuple-element.16), channel_id=1, source_target_pairs={{0,1},{1,2},{2,3},{4,5},{5,6},{6,7},{8,9},{9,10},{10,11},{12,13},{... | collective-permute-start | bytes 27656 | tf_op jit(solution)/shard_map/ppermute | solution.py:18
  48.8 3.8 %collective-permute-start.11 = (f32[18,1,128]{2,1,0:T(1,128)S(1)}, f32[18,1,128]{2,1,0:T(1,128)S(1)}, u32[]{:S(2)}, u32[]{:S(2)}) collective-permute-start(f32[18,1,128]{2,1,0:T(1,128)S(1)} %get-tuple-element.17), channel_id=1, source_target_pairs={{1,0},{2,1},{3,2},{5,4},{6,5},{7,6},{9,8},{10,9},{11,10},{13,12},{... | collective-permute-start | bytes 27656 | tf_op jit(solution)/shard_map/ppermute | solution.py:21
  53.3 17.3 %collective-permute-start.12 = (f32[1,64,128]{2,1,0:T(8,128)S(1)}, f32[1,64,128]{2,1,0:T(8,128)S(1)}, u32[]{:S(2)}, u32[]{:S(2)}) collective-permute-start(f32[1,64,128]{2,1,0:T(8,128)S(1)} %get-tuple-element.32), channel_id=1, source_target_pairs={{0,4},{4,8},{8,12},{12,16},{16,20},{20,24},{24,28},{1,5},{5,9},{9,... | collective-permute-start | bytes 98312 | tf_op jit(solution)/shard_map/ppermute | solution.py:18
  58.2 12.5 %collective-permute-start.13 = (f32[1,64,128]{2,1,0:T(8,128)S(1)}, f32[1,64,128]{2,1,0:T(8,128)S(1)}, u32[]{:S(2)}, u32[]{:S(2)}) collective-permute-start(f32[1,64,128]{2,1,0:T(8,128)S(1)} %get-tuple-element.33), channel_id=1, source_target_pairs={{4,0},{8,4},{12,8},{16,12},{20,16},{24,20},{28,24},{5,1},{9,5},{13... | collective-permute-start | bytes 98312 | tf_op jit(solution)/shard_map/ppermute | solution.py:21
  64.6 17.9 %all-to-all-start = ((s32[8,1,320]{2,1,0:T(1,128)}), s32[8,1,320]{2,1,0:T(1,128)S(1)}, u32[]{:S(2)}, u32[]{:S(2)}) async-start(s32[8,1,320]{2,1,0:T(1,128)} %all_to_all.12), calls=%async_computation | async-start | bytes 24576 | tf_op jit(solution)/shard_map/all_to_all | solution.py:112
  70.6 7.1 %copy-start.5 = (f32[16,64,128]{2,1,0:T(8,128)S(1)}, f32[16,64,128]{2,1,0:T(8,128)}, u32[]{:S(2)}) copy-start(f32[16,64,128]{2,1,0:T(8,128)} %copy-done.4) | copy-start | bytes 1572868
  70.6 7.1 %copy-start.8 = (f32[16,64,128]{2,1,0:T(8,128)S(1)}, f32[16,64,128]{2,1,0:T(8,128)}, u32[]{:S(2)}) copy-start(f32[16,64,128]{2,1,0:T(8,128)} %copy-done.7) | copy-start | bytes 1572868
  70.7 5.1 %collective-permute-start.14 = (f32[18,1,128]{2,1,0:T(1,128)S(1)}, f32[18,1,128]{2,1,0:T(1,128)S(1)}, u32[]{:S(2)}, u32[]{:S(2)}) collective-permute-start(f32[18,1,128]{2,1,0:T(1,128)S(1)} %get-tuple-element.14), channel_id=1, source_target_pairs={{0,1},{1,2},{2,3},{4,5},{5,6},{6,7},{8,9},{9,10},{10,11},{12,13},{... | collective-permute-start | bytes 27656 | tf_op jit(solution)/shard_map/ppermute | solution.py:18
  74.3 3.4 %collective-permute-start.15 = (f32[18,1,128]{2,1,0:T(1,128)S(1)}, f32[18,1,128]{2,1,0:T(1,128)S(1)}, u32[]{:S(2)}, u32[]{:S(2)}) collective-permute-start(f32[18,1,128]{2,1,0:T(1,128)S(1)} %get-tuple-element.15), channel_id=1, source_target_pairs={{1,0},{2,1},{3,2},{5,4},{6,5},{7,6},{9,8},{10,9},{11,10},{13,12},{... | collective-permute-start | bytes 27656 | tf_op jit(solution)/shard_map/ppermute | solution.py:21
  82.6 0.6 copy-start.14
  82.6 53.6 %copy-start.11 = (f32[1,128,128]{2,1,0:T(8,128)S(1)}, f32[1,128,128]{2,1,0:T(8,128)}, u32[]{:S(2)}) copy-start(f32[1,128,128]{2,1,0:T(8,128)} %param.13) | copy-start | bytes 196612
  83.2 38.1 %all-to-all-start.1 = ((f32[8,320,128]{2,1,0:T(8,128)}), f32[8,320,128]{2,1,0:T(8,128)S(1)}, u32[]{:S(2)}, u32[]{:S(2)}) async-start(f32[8,320,128]{2,1,0:T(8,128)} %bitcast.8), calls=%async_computation.1 | async-start | bytes 2621440 | tf_op jit(solution)/shard_map/all_to_all | solution.py:105
  136.2 2.2 %copy-start.12 = (f32[128,128]{1,0:T(8,128)S(1)}, f32[128,128]{1,0:T(8,128)}, u32[]{:S(2)}) copy-start(f32[128,128]{1,0:T(8,128)} %scatter_custom_fusion.2) | copy-start | bytes 196612
  136.2 2.2 %copy-start.13 = (f32[1,128,128]{2,1,0:T(8,128)S(1)}, f32[1,128,128]{2,1,0:T(8,128)}, u32[]{:S(2)}) copy-start(f32[1,128,128]{2,1,0:T(8,128)} %param.12) | copy-start | bytes 196612
  144.1 36.3 %all-to-all-start.2 = ((f32[8,320,128]{2,1,0:T(8,128)}), f32[8,320,128]{2,1,0:T(8,128)S(1)}, u32[]{:S(2)}, u32[]{:S(2)}) async-start(f32[8,320,128]{2,1,0:T(8,128)} %bitcast.76), calls=%async_computation.2 | async-start | bytes 2621440 | tf_op jit(solution)/shard_map/all_to_all | solution.py:123
  185.5 5.0 %collective-permute-start.16 = (f32[1,64,128]{2,1,0:T(8,128)S(1)}, f32[1,64,128]{2,1,0:T(8,128)S(1)}, u32[]{:S(2)}, u32[]{:S(2)}) collective-permute-start(f32[1,64,128]{2,1,0:T(8,128)S(1)} %get-tuple-element.28), channel_id=1, source_target_pairs={{0,4},{4,8},{8,12},{12,16},{16,20},{20,24},{24,28},{1,5},{5,9},{9,... | collective-permute-start | bytes 98312 | tf_op jit(solution)/shard_map/ppermute | solution.py:18
  188.9 10.4 %copy-start.3 = (f32[16,64,128]{2,1,0:T(8,128)S(1)}, f32[16,64,128]{2,1,0:T(8,128)}, u32[]{:S(2)}) copy-start(f32[16,64,128]{2,1,0:T(8,128)} %copy-done.2) | copy-start | bytes 1572868
  188.9 10.4 %copy-start.6 = (f32[16,64,128]{2,1,0:T(8,128)S(1)}, f32[16,64,128]{2,1,0:T(8,128)}, u32[]{:S(2)}) copy-start(f32[16,64,128]{2,1,0:T(8,128)} %copy-done.4) | copy-start | bytes 1572868
  188.9 10.3 %copy-start.9 = (f32[16,64,128]{2,1,0:T(8,128)S(1)}, f32[16,64,128]{2,1,0:T(8,128)}, u32[]{:S(2)}) copy-start(f32[16,64,128]{2,1,0:T(8,128)} %copy-done.7) | copy-start | bytes 1572868
  188.9 5.9 %collective-permute-start.17 = (f32[1,64,128]{2,1,0:T(8,128)S(1)}, f32[1,64,128]{2,1,0:T(8,128)S(1)}, u32[]{:S(2)}, u32[]{:S(2)}) collective-permute-start(f32[1,64,128]{2,1,0:T(8,128)S(1)} %get-tuple-element.29), channel_id=1, source_target_pairs={{4,0},{8,4},{12,8},{16,12},{20,16},{24,20},{28,24},{5,1},{9,5},{13... | collective-permute-start | bytes 98312 | tf_op jit(solution)/shard_map/ppermute | solution.py:21
  194.9 2.8 %collective-permute-start.18 = (f32[18,1,128]{2,1,0:T(1,128)S(1)}, f32[18,1,128]{2,1,0:T(1,128)S(1)}, u32[]{:S(2)}, u32[]{:S(2)}) collective-permute-start(f32[18,1,128]{2,1,0:T(1,128)S(1)} %get-tuple-element.12), channel_id=1, source_target_pairs={{0,1},{1,2},{2,3},{4,5},{5,6},{6,7},{8,9},{9,10},{10,11},{12,13},{... | collective-permute-start | bytes 27656 | tf_op jit(solution)/shard_map/ppermute | solution.py:18
  196.2 3.1 %collective-permute-start.19 = (f32[18,1,128]{2,1,0:T(1,128)S(1)}, f32[18,1,128]{2,1,0:T(1,128)S(1)}, u32[]{:S(2)}, u32[]{:S(2)}) collective-permute-start(f32[18,1,128]{2,1,0:T(1,128)S(1)} %get-tuple-element.13), channel_id=1, source_target_pairs={{1,0},{2,1},{3,2},{5,4},{6,5},{7,6},{9,8},{10,9},{11,10},{13,12},{... | collective-permute-start | bytes 27656 | tf_op jit(solution)/shard_map/ppermute | solution.py:21
  199.9 4.4 %collective-permute-start.20 = (f32[1,64,128]{2,1,0:T(8,128)S(1)}, f32[1,64,128]{2,1,0:T(8,128)S(1)}, u32[]{:S(2)}, u32[]{:S(2)}) collective-permute-start(f32[1,64,128]{2,1,0:T(8,128)S(1)} %get-tuple-element.24), channel_id=1, source_target_pairs={{0,4},{4,8},{8,12},{12,16},{16,20},{20,24},{24,28},{1,5},{5,9},{9,... | collective-permute-start | bytes 98312 | tf_op jit(solution)/shard_map/ppermute | solution.py:18
  202.8 5.9 %collective-permute-start.21 = (f32[1,64,128]{2,1,0:T(8,128)S(1)}, f32[1,64,128]{2,1,0:T(8,128)S(1)}, u32[]{:S(2)}, u32[]{:S(2)}) collective-permute-start(f32[1,64,128]{2,1,0:T(8,128)S(1)} %get-tuple-element.25), channel_id=1, source_target_pairs={{4,0},{8,4},{12,8},{16,12},{20,16},{24,20},{28,24},{5,1},{9,5},{13... | collective-permute-start | bytes 98312 | tf_op jit(solution)/shard_map/ppermute | solution.py:21
  208.7 3.5 %collective-permute-start.22 = (f32[18,1,128]{2,1,0:T(1,128)S(1)}, f32[18,1,128]{2,1,0:T(1,128)S(1)}, u32[]{:S(2)}, u32[]{:S(2)}) collective-permute-start(f32[18,1,128]{2,1,0:T(1,128)S(1)} %get-tuple-element.10), channel_id=1, source_target_pairs={{0,1},{1,2},{2,3},{4,5},{5,6},{6,7},{8,9},{9,10},{10,11},{12,13},{... | collective-permute-start | bytes 27656 | tf_op jit(solution)/shard_map/ppermute | solution.py:18
  210.7 3.9 %collective-permute-start.23 = (f32[18,1,128]{2,1,0:T(1,128)S(1)}, f32[18,1,128]{2,1,0:T(1,128)S(1)}, u32[]{:S(2)}, u32[]{:S(2)}) collective-permute-start(f32[18,1,128]{2,1,0:T(1,128)S(1)} %get-tuple-element.11), channel_id=1, source_target_pairs={{1,0},{2,1},{3,2},{5,4},{6,5},{7,6},{9,8},{10,9},{11,10},{13,12},{... | collective-permute-start | bytes 27656 | tf_op jit(solution)/shard_map/ppermute | solution.py:21
where the time goes:
time: 219 us; the launch traced here: 216 us
  waiting for transfers between devices  86.9 us (40%)
  starting transfers between devices  73.5 us (34%)
  other arithmetic  28 us (13%)
  local copies, waits for them, and re-layouts  27.2 us (12%)
    ppermute x12, starting transfers between devices, extended_2(): lax.ppermute(lax.slice_in_dim(block, block.shape[dim] - width, None, axis...  41.5 us
    all_to_all x1, waiting for transfers between devices, per_device(): lax.all_to_all(replies, 'bulk', split_axis=0, concat_axis=0, tiled=True)  32.1 us
    all_to_all x1, waiting for transfers between devices, per_device(): lax.all_to_all(outgoing.reshape(bulk_count, capacity, depth_cells), 'bulk...  29.3 us
    ppermute x12, waiting for transfers between devices, extended_2(): lax.ppermute(lax.slice_in_dim(block, 0, width, axis=dim), axis, backward)  24.9 us
    ppermute x12, starting transfers between devices, extended_2(): lax.ppermute(lax.slice_in_dim(block, 0, width, axis=dim), axis, backward)  15.8 us
    scatter-add x1, other arithmetic, per_device(): jax.ops.segment_sum(arrived.reshape(-1, depth_cells), flat_labels, num_se...  14.9 us
    all_to_all x1, starting transfers between devices, per_device(): lax.all_to_all(outgoing.reshape(bulk_count, capacity, depth_cells), 'bulk...  5.98 us
    all_to_all x1, starting transfers between devices, per_device(): lax.all_to_all(labels.reshape(bulk_count, capacity), 'bulk', split_axis=0...  5.95 us
  transfers between devices with their start and end apart: 27, of which 13 were waited for; matrix products, arithmetic and copies ran while one was open for 9% of the time, Pallas kernels for 0%

commit v1 on v0

v1 whole, which is shorter than its diff:
```python
import functools

import jax
import jax.numpy as jnp
from jax import lax
from jax.experimental import pallas as pl
from jax.experimental.pallas import tpu as pltpu
from jax.sharding import PartitionSpec as P

SWEEPS = 2
COARSE_SWEEPS = 3
DAMPING = 0.8
PAD = 8
PIECES = 3


def pieces_of(values):
    terms = []
    for index in range(PIECES):
        term = values.astype(jnp.bfloat16)
        terms.append(term)
        if index < PIECES - 1:
            values = values - term.astype(jnp.float32)
    return jnp.concatenate(terms, axis=1)


def joined(product, width):
    total = product[:, :width]
    for index in range(1, PIECES):
        total = total + product[:, index * width : (index + 1) * width]
    return total


def each(count, body):
    if count <= 8:
        for index in range(count):
            body(index)
    else:
        def step(index, carry):
            body(index)
            return carry

        lax.fori_loop(0, count, step, 0)


def kernel(
    nb, ns, key_ref, p_ref, r_ref, k_ref, leak_ref, link_ref, out_ref,
    v, k, rhs, fw, fs, fn, fl, fu, diag, dinv, ysend, yhalo, kysend, kyhalo,
    spread, gather, keycol, rp, part, arrived, corr, acc,
    load_sem, send_sem, recv_sem, ksend_sem, krecv_sem,
    rs_send, rs_recv, ag_send, ag_recv,
):
    cx, cy, nz = out_ref.shape
    cr = leak_ref.shape[0]
    rows = cx * cy
    b = lax.axis_index("bulk")
    s = lax.axis_index("slab")
    body_rows = pl.ds(PAD, cy)

    loads = [
        pltpu.make_async_copy(p_ref, v.at[0, pl.ds(1, cx), body_rows], load_sem.at[0]),
        pltpu.make_async_copy(k_ref, k.at[pl.ds(1, cx), body_rows], load_sem.at[1]),
        pltpu.make_async_copy(r_ref, rhs, load_sem.at[2]),
    ]
    for load in loads:
        load.start()

    has = (b > 0, b < nb - 1, s > 0, s < ns - 1)

    barrier = pltpu.get_barrier_semaphore()

    def greet(j):
        pl.semaphore_signal(
            barrier, inc=1, device_id={"bulk": lax.rem(b + j + 1, nb)},
            device_id_type=pl.DeviceIdType.MESH,
        )

    each(nb - 1, greet)
    for there, step in ((has[2], -1), (has[3], 1)):
        @pl.when(there)
        def _(step=step):
            pl.semaphore_signal(
                barrier, inc=1, device_id={"slab": s + step},
                device_id_type=pl.DeviceIdType.MESH,
            )

    zlane = lax.broadcasted_iota(jnp.int32, (cy, nz), 1)
    first, last = zlane == 0, zlane == nz - 1

    plane0 = jnp.zeros((cy, nz), jnp.float32)
    for there, place in ((has[0], 0), (has[1], cx + 1)):
        @pl.when(jnp.logical_not(there))
        def _(place=place):
            k[place, PAD : PAD + cy] = plane0
            for stage in range(2 * SWEEPS + 1):
                v[stage, place, PAD : PAD + cy] = plane0
    for there, side in ((has[2], 0), (has[3], 1)):
        @pl.when(jnp.logical_not(there))
        def _(side=side):
            kyhalo[side] = jnp.zeros((cx, nz), jnp.float32)
            for stage in range(2 * SWEEPS + 1):
                yhalo[stage, side] = jnp.zeros((cx, nz), jnp.float32)

    lanes = key_ref.shape[1]
    for a in range(key_ref.shape[0]):
        wide = jnp.broadcast_to(key_ref[a : a + 1, :], (lanes, lanes)).astype(jnp.float32)
        keycol[a * lanes : (a + 1) * lanes, :] = wide.T.astype(jnp.int32)

    def onehots(j):
        base = lax.rem(b + j + 1, nb) * cr
        down = lax.broadcasted_iota(jnp.int32, (cr, lanes), 0) + base
        across = lax.broadcasted_iota(jnp.int32, (lanes, cr), 1) + base
        for a in range(key_ref.shape[0]):
            hit = jnp.broadcast_to(key_ref[a : a + 1, :], (cr, lanes)) == down
            spread[j, :, a * lanes : (a + 1) * lanes] = jnp.where(hit, 1.0, 0.0).astype(jnp.bfloat16)
            hit = keycol[a * lanes : (a + 1) * lanes, :cr] == across
            gather[j, a * lanes : (a + 1) * lanes, :] = jnp.where(hit, 1.0, 0.0).astype(jnp.bfloat16)

    def x_copies(ref, sends, recvs, lead):
        def made(source, target, index, step):
            return pltpu.make_async_remote_copy(
                src_ref=ref.at[*lead, source, body_rows], dst_ref=ref.at[*lead, target, body_rows],
                send_sem=sends.at[*lead, index], recv_sem=recvs.at[*lead, index],
                device_id={"bulk": b + step}, device_id_type=pl.DeviceIdType.MESH,
            )
        return made(cx, 0, 0, 1), made(1, cx + 1, 1, -1)

    def y_copies(source, target, sends, recvs, lead):
        def made(side, index, step):
            return pltpu.make_async_remote_copy(
                src_ref=source.at[*lead, side], dst_ref=target.at[*lead, 1 - side],
                send_sem=sends.at[*lead, index], recv_sem=recvs.at[*lead, index],
                device_id={"slab": s + step}, device_id_type=pl.DeviceIdType.MESH,
            )
        return made(1, 2, 1), made(0, 3, -1)

    def copies_of(stage):
        lead = (stage,)
        return x_copies(v, send_sem, recv_sem, lead) + y_copies(ysend, yhalo, send_sem, recv_sem, lead)

    def k_copies():
        return x_copies(k, ksend_sem, krecv_sem, ()) + y_copies(kysend, kyhalo, ksend_sem, krecv_sem, ())

    to = (has[1], has[0], has[3], has[2])
    origin = (has[0], has[1], has[2], has[3])

    def start_all(copies):
        for there, copy in zip(to, copies):
            pl.when(there)(copy.start)

    def recv_all(copies):
        for there, copy in zip(origin, copies):
            pl.when(there)(copy.wait_recv)

    def send_all(copies):
        for there, copy in zip(to, copies):
            pl.when(there)(copy.wait_send)

    def stage_rows(ref, lead, target):
        for x in range(cx):
            target[*lead, 0, x : x + 1] = ref[*lead, x + 1, PAD : PAD + 1]
            target[*lead, 1, x : x + 1] = ref[*lead, x + 1, PAD + cy - 1 : PAD + cy]

    def place_rows(source, lead, ref):
        for x in range(cx):
            ref[*lead, x + 1, PAD - 1 : PAD] = source[*lead, 0, x : x + 1]
            ref[*lead, x + 1, PAD + cy : PAD + cy + 1] = source[*lead, 1, x : x + 1]

    def planes(body):
        def step(x, carry):
            body(x)
            return carry

        lax.fori_loop(0, cx, step, 0)

    loads[0].wait()
    stage_rows(v, (0,), ysend)
    loads[1].wait()
    stage_rows(k, (), kysend)

    pl.semaphore_wait(barrier, nb - 1 + has[2].astype(jnp.int32) + has[3].astype(jnp.int32))

    start_all(k_copies())
    start_all(copies_of(0))
    each(nb, onehots)
    loads[2].wait()
    recv_all(k_copies())
    place_rows(kyhalo, (), k)

    def coefficients(x):
        here = k[x + 1, PAD : PAD + cy]
        west = 0.5 * (here + k[x, PAD : PAD + cy])
        east = 0.5 * (here + k[x + 2, PAD : PAD + cy])
        south = 0.5 * (here + k[x + 1, PAD - 1 : PAD - 1 + cy])
        north = 0.5 * (here + k[x + 1, PAD + 1 : PAD + 1 + cy])
        lower = 0.5 * (here + jnp.where(first, 0.0, pltpu.roll(here, 1, 1)))
        upper = 0.5 * (here + jnp.where(last, 0.0, pltpu.roll(here, nz - 1, 1)))
        total = west + east + south + north + lower + upper
        fw[x] = west
        fw[x + 1] = east
        fs[x] = south
        fn[x] = north
        fl[x] = jnp.where(first, 0.0, lower)
        fu[x] = jnp.where(last, 0.0, upper)
        diag[x] = total
        dinv[x] = DAMPING / total

    planes(coefficients)

    def around(stage, x):
        here = v[stage, x + 1, PAD : PAD + cy]
        total = rhs[x] + fw[x] * v[stage, x, PAD : PAD + cy] + fw[x + 1] * v[stage, x + 2, PAD : PAD + cy]
        total = total + fs[x] * v[stage, x + 1, PAD - 1 : PAD - 1 + cy]
        total = total + fn[x] * v[stage, x + 1, PAD + 1 : PAD + 1 + cy]
        total = total + fl[x] * pltpu.roll(here, 1, 1) + fu[x] * pltpu.roll(here, nz - 1, 1)
        return total, here

    def halo_in(stage):
        recv_all(copies_of(stage))
        place_rows(yhalo, (stage,), v)

    def halo_out(stage):
        stage_rows(v, (stage,), ysend)
        start_all(copies_of(stage))

    def smooth(stage):
        def body(x):
            total, here = around(stage, x)
            v[stage + 1, x + 1, PAD : PAD + cy] = (1 - DAMPING) * here + dinv[x] * total

        planes(body)

    for stage in range(SWEEPS):
        halo_in(stage)
        smooth(stage)
        halo_out(stage + 1)

    halo_in(SWEEPS)

    def residual(x):
        total, here = around(SWEEPS, x)
        rp[pl.ds(pl.multiple_of(x * cy, cy), cy), :] = pieces_of(total - diag[x] * here)

    planes(residual)

    def rs_copy(j):
        return pltpu.make_async_remote_copy(
            src_ref=part.at[j], dst_ref=arrived.at[j],
            send_sem=rs_send.at[j], recv_sem=rs_recv.at[j],
            device_id={"bulk": lax.rem(b + j + 1, nb)}, device_id_type=pl.DeviceIdType.MESH,
        )

    group = 4 if nb % 4 == 0 else 1

    def scatter(g):
        hot = spread[pl.ds(g * group, group)].reshape(group * cr, rows)
        product = jnp.dot(hot, rp[...], preferred_element_type=jnp.float32)
        part[pl.ds(g * group, group)] = joined(product, nz).reshape(group, cr, nz)

    for g in range(nb // group) if nb // group <= 4 else ():
        scatter(g)
        for j in range(g * group, min((g + 1) * group, nb - 1)):
            rs_copy(j).start()
    if nb // group > 4:
        each(nb // group, scatter)
        each(nb - 1, lambda j: rs_copy(j).start())

    zc = lax.broadcasted_iota(jnp.int32, (cr, nz), 1)
    link = link_ref[...]
    below = jnp.where(zc == 0, 0.0, pltpu.roll(link, 1, 1))
    cinv = DAMPING / (leak_ref[...] + link + below)
    above = jnp.where(zc == nz - 1, 0.0, link)

    each(nb - 1, lambda j: rs_copy(j).wait_recv())
    if nb <= 8:
        coarse = part[nb - 1]
        for j in range(nb - 1):
            coarse = coarse + arrived[j]
    else:
        coarse = lax.fori_loop(0, nb - 1, lambda j, total: total + arrived[j], part[nb - 1])

    u = cinv * coarse
    for sweep in range(COARSE_SWEEPS - 1):
        u = (1 - DAMPING) * u + cinv * (
            coarse + above * pltpu.roll(u, nz - 1, 1) + below * pltpu.roll(u, 1, 1)
        )
    corr[nb - 1] = u

    def ag_copy(j):
        return pltpu.make_async_remote_copy(
            src_ref=corr.at[nb - 1], dst_ref=corr.at[nb - 2 - j],
            send_sem=ag_send.at[nb - 2 - j], recv_sem=ag_recv.at[nb - 2 - j],
            device_id={"bulk": lax.rem(b + j + 1, nb)}, device_id_type=pl.DeviceIdType.MESH,
        )

    each(nb - 1, lambda j: ag_copy(j).start())

    def collect(g, fresh):
        values = pieces_of(corr[pl.ds(g * group, group)].reshape(group * cr, nz))
        hot = jnp.concatenate([gather[g * group + i] for i in range(group)], axis=1)
        product = joined(jnp.dot(hot, values, preferred_element_type=jnp.float32), nz)
        acc[...] = product if fresh else acc[...] + product

    if nb // group <= 4:
        for g in range(nb // group):
            for j in range(g * group, min((g + 1) * group, nb - 1)):
                ag_copy(nb - 2 - j).wait_recv()
            collect(g, g == 0)
    else:
        each(nb - 1, lambda j: ag_copy(j).wait_recv())
        acc[...] = jnp.zeros((rows, nz), jnp.float32)
        each(nb // group, lambda g: collect(g, False))

    def corrected(x):
        v[SWEEPS + 1, x + 1, PAD : PAD + cy] = (
            v[SWEEPS, x + 1, PAD : PAD + cy] + acc[pl.ds(pl.multiple_of(x * cy, cy), cy), :]
        )

    planes(corrected)
    halo_out(SWEEPS + 1)

    for stage in range(SWEEPS + 1, 2 * SWEEPS):
        halo_in(stage)
        smooth(stage)
        halo_out(stage + 1)

    halo_in(2 * SWEEPS)

    def finish(x):
        total, here = around(2 * SWEEPS, x)
        out_ref[x] = (1 - DAMPING) * here + dinv[x] * total

    planes(finish)

    send_all(k_copies())
    for stage in range(2 * SWEEPS + 1):
        send_all(copies_of(stage))
    each(nb - 1, lambda j: rs_copy(j).wait_send())
    each(nb - 1, lambda j: ag_copy(j).wait_send())


def per_device(nb, ns, pressure, rhs, kappa, owner, coarse_row, coarse_leak, coarse_link):
    cx, cy, nz = pressure.shape
    cr = coarse_leak.shape[1]
    rows = cx * cy
    lanes = 128
    key = owner.reshape(rows // lanes, lanes) * cr + coarse_row.reshape(rows // lanes, lanes)
    stages = 2 * SWEEPS + 1
    f32, bf16 = jnp.float32, jnp.bfloat16
    block = (cx, cy, nz)
    padded = (cx + 2, cy + 2 * PAD, nz)
    vmem = pl.BlockSpec(memory_space=pltpu.VMEM)
    hbm = pl.BlockSpec(memory_space=pl.ANY)
    dma = pltpu.SemaphoreType.DMA
    return pl.pallas_call(
        functools.partial(kernel, nb, ns),
        out_shape=jax.ShapeDtypeStruct(block, f32),
        in_specs=[vmem, hbm, hbm, hbm, vmem, vmem],
        out_specs=vmem,
        scratch_shapes=[
            pltpu.VMEM((stages,) + padded, f32),
            pltpu.VMEM(padded, f32),
            pltpu.VMEM(block, f32),
            pltpu.VMEM((cx + 1, cy, nz), f32),
            pltpu.VMEM(block, f32),
            pltpu.VMEM(block, f32),
            pltpu.VMEM(block, f32),
            pltpu.VMEM(block, f32),
            pltpu.VMEM(block, f32),
            pltpu.VMEM(block, f32),
            pltpu.VMEM((stages, 2, cx, nz), f32),
            pltpu.VMEM((stages, 2, cx, nz), f32),
            pltpu.VMEM((2, cx, nz), f32),
            pltpu.VMEM((2, cx, nz), f32),
            pltpu.VMEM((nb, cr, rows), bf16),
            pltpu.VMEM((nb, rows, cr), bf16),
            pltpu.VMEM((rows, lanes), jnp.int32),
            pltpu.VMEM((rows, PIECES * nz), bf16),
            pltpu.VMEM((nb, cr, nz), f32),
            pltpu.VMEM((nb, cr, nz), f32),
            pltpu.VMEM((nb, cr, nz), f32),
            pltpu.VMEM((rows, nz), f32),
            dma((3,)),
            dma((stages, 4)),
            dma((stages, 4)),
            dma((4,)),
            dma((4,)),
            dma((nb,)),
            dma((nb,)),
            dma((nb,)),
            dma((nb,)),
        ],
        compiler_params=pltpu.CompilerParams(
            collective_id=0, has_side_effects=True, vmem_limit_bytes=60 * 2**20
        ),
    )(key, pressure, rhs, kappa, coarse_leak[0], coarse_link[0])


def solution(mesh):
    return jax.shard_map(
        functools.partial(per_device, mesh.shape["bulk"], mesh.shape["slab"]),
        mesh=mesh,
        in_specs=(
            P("bulk", "slab", None),
            P("bulk", "slab", None),
            P("bulk", "slab", None),
            P("slab", "bulk", None, None),
            P("slab", "bulk", None),
            P("slab", "bulk", None),
            P("slab", "bulk", None),
        ),
        out_specs=P("bulk", "slab", None),
        check_vma=False,
    )
```

time: 219 us -> 64.5 us (0.29)
  the two profiles are of different devices: /device:TPU:0 before, /device:TPU:18 now
where the time goes in v1:
time: 64.5 us; the launch traced here: 64.2 us
  Pallas kernels  60.3 us (93%)
  local copies, waits for them, and re-layouts  3.25 us (5%)
    pallas_call x1, Pallas kernels, per_device(): pl.pallas_call(functools.partial(kernel, nb, ns), out_shape=jax.ShapeDtyp...  60.3 us
    unnamed x5, local copies, waits for them, and re-layouts  3.25 us

profile of v1, /device:TPU:18, one launch (start us, length us, event | category | flops | bytes accessed | tf_op | source)
XLA Modules:
  0.0 64.2 jit_solution(731044991176637625)
XLA Ops:
  0.0 0.0 copy-start.1
  0.0 0.7 %copy-done.1 = s32[1,1,1024,1]{2,3,1,0:T(1,128)S(1)} copy-done((s32[1,1,1024,1]{2,3,1,0:T(1,128)S(1)}, s32[1,1,1024,1]{2,3,1,0:T(1,128)}, u32[]{:S(2)}) %copy-start.1) | copy-done | bytes 4120
  0.7 0.0 copy-start
  0.7 0.7 %copy-done = s32[1,1,1024]{2,1,0:T(1,128)S(1)} copy-done((s32[1,1,1024]{2,1,0:T(1,128)S(1)}, s32[1,1,1024]{2,1,0:T(1,128)}, u32[]{:S(2)}) %copy-start) | copy-done | bytes 4120
  1.4 0.6 add.3.key_ref
  2.0 60.3 %shard_map.73 = f32[16,64,128]{2,1,0:T(8,128)} custom-call(s32[8,128]{1,0:T(8,128)} %add.3.key_ref, f32[16,64,128]{2,1,0:T(8,128)} %p_ref.1, f32[16,64,128]{2,1,0:T(8,128)} %r_ref.1, f32[16,64,128]{2,1,0:T(8,128)} %k_ref.1, f32[128,128]{1,0:T(8,128)} %bitcast.4, f32[128,128]{1,0:T(8,128)} %bitcast.5), custom_call_target="tpu_custom_call" | custom-call | tf_op jit(solution)/shard_map/pallas_call | solution.py:355
  62.3 1.9 %copy.9 = f32[16,64,128]{2,1,0:T(8,128)} copy(f32[16,64,128]{2,1,0:T(8,128)} %shard_map.73) | data formatting | bytes 1048576
  (1 shorter events, 0.0 us)
Async XLA Ops:
  0.0 0.7 %copy-start.1 = (s32[1,1,1024,1]{2,3,1,0:T(1,128)S(1)}, s32[1,1,1024,1]{2,3,1,0:T(1,128)}, u32[]{:S(2)}) copy-start(s32[1,1,1024,1]{2,3,1,0:T(1,128)} %param.10) | copy-start | bytes 12292
  0.7 0.7 %copy-start = (s32[1,1,1024]{2,1,0:T(1,128)S(1)}, s32[1,1,1024]{2,1,0:T(1,128)}, u32[]{:S(2)}) copy-start(s32[1,1,1024]{2,1,0:T(1,128)} %param.11) | copy-start | bytes 12292

commit v2 on v1

--- a/solution.py
+++ b/solution.py
@@ -44,11 +44,11 @@
 
 
 def kernel(
-    nb, ns, key_ref, p_ref, r_ref, k_ref, leak_ref, link_ref, out_ref,
-    v, k, rhs, fw, fs, fn, fl, fu, diag, dinv, ysend, yhalo, kysend, kyhalo,
-    spread, gather, keycol, rp, part, arrived, corr, acc,
+    nb, ns, owner_ref, row_ref, p_ref, r_ref, k_ref, leak_hbm, link_hbm, out_hbm,
+    key_ref, row_key, leak_ref, link_ref, out_ref, v, k, rhs, fw, fs, fn, fl, fu, diag, dinv, ysend, yhalo, kysend, kyhalo,
+    spread, gather, keycol, rp, part, crossed, arrived, corr, acc,
     load_sem, send_sem, recv_sem, ksend_sem, krecv_sem,
-    rs_send, rs_recv, ag_send, ag_recv,
+    rs_send, rs_recv, ag_send, ag_recv, px_send, px_recv, cx_send, cx_recv, out_sem,
 ):
     cx, cy, nz = out_ref.shape
     cr = leak_ref.shape[0]
@@ -60,7 +60,11 @@
     loads = [
         pltpu.make_async_copy(p_ref, v.at[0, pl.ds(1, cx), body_rows], load_sem.at[0]),
         pltpu.make_async_copy(k_ref, k.at[pl.ds(1, cx), body_rows], load_sem.at[1]),
+        pltpu.make_async_copy(owner_ref, key_ref, load_sem.at[3]),
+        pltpu.make_async_copy(row_ref, row_key, load_sem.at[4]),
         pltpu.make_async_copy(r_ref, rhs, load_sem.at[2]),
+        pltpu.make_async_copy(leak_hbm, leak_ref, load_sem.at[5]),
+        pltpu.make_async_copy(link_hbm, link_ref, load_sem.at[6]),
     ]
     for load in loads:
         load.start()
@@ -88,26 +92,36 @@
     first, last = zlane == 0, zlane == nz - 1
 
     plane0 = jnp.zeros((cy, nz), jnp.float32)
-    for there, place in ((has[0], 0), (has[1], cx + 1)):
+    for there, end in ((has[0], 0), (has[1], cx + 1)):
         @pl.when(jnp.logical_not(there))
-        def _(place=place):
-            k[place, PAD : PAD + cy] = plane0
+        def _(end=end):
+            k[end, PAD : PAD + cy] = plane0
             for stage in range(2 * SWEEPS + 1):
-                v[stage, place, PAD : PAD + cy] = plane0
-    for there, side in ((has[2], 0), (has[3], 1)):
+                v[stage, end, PAD : PAD + cy] = plane0
+    for there, edge in ((has[2], 0), (has[3], 1)):
         @pl.when(jnp.logical_not(there))
-        def _(side=side):
-            kyhalo[side] = jnp.zeros((cx, nz), jnp.float32)
+        def _(edge=edge):
+            kyhalo[edge] = jnp.zeros((cx, nz), jnp.float32)
             for stage in range(2 * SWEEPS + 1):
-                yhalo[stage, side] = jnp.zeros((cx, nz), jnp.float32)
-
+                yhalo[stage, edge] = jnp.zeros((cx, nz), jnp.float32)
+
+    half = nb // 2
+    place, side = b // 2, lax.rem(b, 2)
+    other = 1 - side
     lanes = key_ref.shape[1]
+    loads[2].wait()
+    loads[3].wait()
+    key_ref[...] = key_ref[...] * cr + row_key[...]
+
+    def pair_at(q):
+        return lax.rem(place + q + 1, half) * 2
+
     for a in range(key_ref.shape[0]):
         wide = jnp.broadcast_to(key_ref[a : a + 1, :], (lanes, lanes)).astype(jnp.float32)
         keycol[a * lanes : (a + 1) * lanes, :] = wide.T.astype(jnp.int32)
 
     def onehots(j):
-        base = lax.rem(b + j + 1, nb) * cr
+        base = (pair_at(j) + jnp.where(j < half, side, other)) * cr
         down = lax.broadcasted_iota(jnp.int32, (cr, lanes), 0) + base
         across = lax.broadcasted_iota(jnp.int32, (lanes, cr), 1) + base
         for a in range(key_ref.shape[0]):
@@ -171,7 +185,7 @@
             body(x)
             return carry
 
-        lax.fori_loop(0, cx, step, 0)
+        lax.fori_loop(0, cx, step, 0, unroll=4)
 
     loads[0].wait()
     stage_rows(v, (0,), ysend)
@@ -183,7 +197,7 @@
     start_all(k_copies())
     start_all(copies_of(0))
     each(nb, onehots)
-    loads[2].wait()
+    loads[4].wait()
     recv_all(k_copies())
     place_rows(kyhalo, (), k)
 
@@ -243,73 +257,98 @@
 
     planes(residual)
 
-    def rs_copy(j):
+    def pair_copy(source, target, q, sends, recvs):
         return pltpu.make_async_remote_copy(
-            src_ref=part.at[j], dst_ref=arrived.at[j],
-            send_sem=rs_send.at[j], recv_sem=rs_recv.at[j],
-            device_id={"bulk": lax.rem(b + j + 1, nb)}, device_id_type=pl.DeviceIdType.MESH,
-        )
-
-    group = 4 if nb % 4 == 0 else 1
-
-    def scatter(g):
-        hot = spread[pl.ds(g * group, group)].reshape(group * cr, rows)
+            src_ref=source, dst_ref=target, send_sem=sends.at[q], recv_sem=recvs.at[q],
+            device_id={"bulk": 2 * place + other}, device_id_type=pl.DeviceIdType.MESH,
+        )
+
+    def far_copy(source, target, q, slot, sends, recvs):
+        return pltpu.make_async_remote_copy(
+            src_ref=source, dst_ref=target, send_sem=sends.at[slot], recv_sem=recvs.at[slot],
+            device_id={"bulk": pair_at(q) + side}, device_id_type=pl.DeviceIdType.MESH,
+        )
+
+    def px_copy(q):
+        return pair_copy(part.at[half + q], crossed.at[q], q, px_send, px_recv)
+
+    def rs_copy(q):
+        return far_copy(part.at[q], arrived.at[q], q, q, rs_send, rs_recv)
+
+    group = 4 if half % 4 == 0 else 1
+
+    def scatter(first_slot):
+        hot = spread[pl.ds(first_slot, group)].reshape(group * cr, rows)
         product = jnp.dot(hot, rp[...], preferred_element_type=jnp.float32)
-        part[pl.ds(g * group, group)] = joined(product, nz).reshape(group, cr, nz)
-
-    for g in range(nb // group) if nb // group <= 4 else ():
-        scatter(g)
-        for j in range(g * group, min((g + 1) * group, nb - 1)):
-            rs_copy(j).start()
-    if nb // group > 4:
-        each(nb // group, scatter)
-        each(nb - 1, lambda j: rs_copy(j).start())
-
+        part[pl.ds(first_slot, group)] = joined(product, nz).reshape(group, cr, nz)
+
+    def scatter_across(g):
+        scatter(half + g * group)
+        each(group, lambda i: px_copy(g * group + i).start())
+
+    each(half // group, scatter_across)
+    each(half // group, lambda g: scatter(g * group))
+
+    loads[5].wait()
+    loads[6].wait()
     zc = lax.broadcasted_iota(jnp.int32, (cr, nz), 1)
     link = link_ref[...]
     below = jnp.where(zc == 0, 0.0, pltpu.roll(link, 1, 1))
     cinv = DAMPING / (leak_ref[...] + link + below)
     above = jnp.where(zc == nz - 1, 0.0, link)
 
-    each(nb - 1, lambda j: rs_copy(j).wait_recv())
-    if nb <= 8:
-        coarse = part[nb - 1]
-        for j in range(nb - 1):
-            coarse = coarse + arrived[j]
+    def pass_on(q):
+        px_copy(q).wait_recv()
+        part[q] = part[q] + crossed[q]
+        rs_copy(q).start()
+
+    each(half - 1, pass_on)
+    px_copy(half - 1).wait_recv()
+    coarse = part[half - 1] + crossed[half - 1]
+    if half <= 8:
+        for q in range(half - 1):
+            rs_copy(q).wait_recv()
+            coarse = coarse + arrived[q]
     else:
-        coarse = lax.fori_loop(0, nb - 1, lambda j, total: total + arrived[j], part[nb - 1])
+        each(half - 1, lambda q: rs_copy(q).wait_recv())
+        coarse = lax.fori_loop(0, half - 1, lambda q, total: total + arrived[q], coarse)
 
     u = cinv * coarse
     for sweep in range(COARSE_SWEEPS - 1):
         u = (1 - DAMPING) * u + cinv * (
             coarse + above * pltpu.roll(u, nz - 1, 1) + below * pltpu.roll(u, 1, 1)
         )
-    corr[nb - 1] = u
-
-    def ag_copy(j):
-        return pltpu.make_async_remote_copy(
-            src_ref=corr.at[nb - 1], dst_ref=corr.at[nb - 2 - j],
-            send_sem=ag_send.at[nb - 2 - j], recv_sem=ag_recv.at[nb - 2 - j],
-            device_id={"bulk": lax.rem(b + j + 1, nb)}, device_id_type=pl.DeviceIdType.MESH,
-        )
-
-    each(nb - 1, lambda j: ag_copy(j).start())
-
-    def collect(g, fresh):
-        values = pieces_of(corr[pl.ds(g * group, group)].reshape(group * cr, nz))
-        hot = jnp.concatenate([gather[g * group + i] for i in range(group)], axis=1)
+    corr[half - 1] = u
+
+    def ag_copy(q):
+        slot = half - 2 - q
+        return far_copy(corr.at[half - 1], corr.at[slot], q, slot, ag_send, ag_recv)
+
+    def cx_copy(q):
+        return pair_copy(corr.at[q], corr.at[half + q], q, cx_send, cx_recv)
+
+    each(half - 1, lambda q: ag_copy(q).start())
+    cx_copy(half - 1).start()
+
+    def hand_over(q):
+        ag_copy(half - 2 - q).wait_recv()
+        cx_copy(q).start()
+
+    each(half - 1, hand_over)
+
+    def collect(first_slot, fresh):
+        values = pieces_of(corr[pl.ds(first_slot, group)].reshape(group * cr, nz))
+        hot = jnp.concatenate([gather[first_slot + i] for i in range(group)], axis=1)
         product = joined(jnp.dot(hot, values, preferred_element_type=jnp.float32), nz)
         acc[...] = product if fresh else acc[...] + product
 
-    if nb // group <= 4:
-        for g in range(nb // group):
-            for j in range(g * group, min((g + 1) * group, nb - 1)):
-                ag_copy(nb - 2 - j).wait_recv()
-            collect(g, g == 0)
+    if half == group:
+        collect(0, True)
     else:
-        each(nb - 1, lambda j: ag_copy(j).wait_recv())
         acc[...] = jnp.zeros((rows, nz), jnp.float32)
-        each(nb // group, lambda g: collect(g, False))
+        each(half // group, lambda g: collect(g * group, False))
+    each(half, lambda q: cx_copy(q).wait_recv())
+    each(half // group, lambda g: collect(half + g * group, False))
 
     def corrected(x):
         v[SWEEPS + 1, x + 1, PAD : PAD + cy] = (
@@ -331,12 +370,31 @@
         out_ref[x] = (1 - DAMPING) * here + dinv[x] * total
 
     planes(finish)
+    result = pltpu.make_async_copy(out_ref, out_hbm, out_sem)
+    result.start()
 
     send_all(k_copies())
     for stage in range(2 * SWEEPS + 1):
         send_all(copies_of(stage))
-    each(nb - 1, lambda j: rs_copy(j).wait_send())
-    each(nb - 1, lambda j: ag_copy(j).wait_send())
+    each(half, lambda q: px_copy(q).wait_send())
+    each(half, lambda q: cx_copy(q).wait_send())
+    each(half - 1, lambda q: rs_copy(q).wait_send())
+    each(half - 1, lambda q: ag_copy(q).wait_send())
+    result.wait()
+
+
+def hand_back(parts, source, target, sems):
+    size = source.shape[0] // parts
+    copies = [
+        pltpu.make_async_copy(
+            source.at[pl.ds(i * size, size)], target.at[pl.ds(i * size, size)], sems.at[i]
+        )
+        for i in range(parts)
+    ]
+    for copy in copies:
+        copy.start()
+    for copy in copies:
+        copy.wait()
 
 
 def per_device(nb, ns, pressure, rhs, kappa, owner, coarse_row, coarse_leak, coarse_link):
@@ -344,7 +402,8 @@
     cr = coarse_leak.shape[1]
     rows = cx * cy
     lanes = 128
-    key = owner.reshape(rows // lanes, lanes) * cr + coarse_row.reshape(rows // lanes, lanes)
+    keys = (rows // lanes, lanes)
+    parts = 4 if cx % 4 == 0 else 1
     stages = 2 * SWEEPS + 1
     f32, bf16 = jnp.float32, jnp.bfloat16
     block = (cx, cy, nz)
@@ -352,12 +411,17 @@
     vmem = pl.BlockSpec(memory_space=pltpu.VMEM)
     hbm = pl.BlockSpec(memory_space=pl.ANY)
     dma = pltpu.SemaphoreType.DMA
-    return pl.pallas_call(
+    result = pl.pallas_call(
         functools.partial(kernel, nb, ns),
         out_shape=jax.ShapeDtypeStruct(block, f32),
-        in_specs=[vmem, hbm, hbm, hbm, vmem, vmem],
-        out_specs=vmem,
+        in_specs=[hbm] * 7,
+        out_specs=hbm,
         scratch_shapes=[
+            pltpu.VMEM(keys, jnp.int32),
+            pltpu.VMEM(keys, jnp.int32),
+            pltpu.VMEM((cr, nz), f32),
+            pltpu.VMEM((cr, nz), f32),
+            pltpu.VMEM(block, f32),
             pltpu.VMEM((stages,) + padded, f32),
             pltpu.VMEM(padded, f32),
             pltpu.VMEM(block, f32),
@@ -377,23 +441,40 @@
             pltpu.VMEM((rows, lanes), jnp.int32),
             pltpu.VMEM((rows, PIECES * nz), bf16),
             pltpu.VMEM((nb, cr, nz), f32),
-            pltpu.VMEM((nb, cr, nz), f32),
+            pltpu.VMEM((nb // 2, cr, nz), f32),
+            pltpu.VMEM((nb // 2, cr, nz), f32),
             pltpu.VMEM((nb, cr, nz), f32),
             pltpu.VMEM((rows, nz), f32),
-            dma((3,)),
+            dma((7,)),
             dma((stages, 4)),
             dma((stages, 4)),
             dma((4,)),
             dma((4,)),
-            dma((nb,)),
-            dma((nb,)),
-            dma((nb,)),
-            dma((nb,)),
+            dma((nb // 2,)),
+            dma((nb // 2,)),
+            dma((nb // 2,)),
+            dma((nb // 2,)),
+            dma((nb // 2,)),
+            dma((nb // 2,)),
+            dma((nb // 2,)),
+            dma((nb // 2,)),
+            dma,
         ],
         compiler_params=pltpu.CompilerParams(
             collective_id=0, has_side_effects=True, vmem_limit_bytes=60 * 2**20
         ),
-    )(key, pressure, rhs, kappa, coarse_leak[0], coarse_link[0])
+    )(
+        owner.reshape(keys), coarse_row.reshape(keys), pressure, rhs, kappa,
+        coarse_leak[0], coarse_link[0],
+    )
+    return pl.pallas_call(
+        functools.partial(hand_back, parts),
+        out_shape=jax.ShapeDtypeStruct(block, f32),
+        in_specs=[hbm],
+        out_specs=hbm,
+        scratch_shapes=[dma((parts,))],
+        compiler_params=pltpu.CompilerParams(vmem_limit_bytes=60 * 2**20),
+    )(result)
 
 
 def solution(mesh):

time: 64.5 us -> 68.9 us (1.068)
  the two profiles are of different devices: /device:TPU:18 before, /device:TPU:0 now
where the time goes in v2:
time: 68.9 us; the launch traced here: 68.7 us
  Pallas kernels  68.7 us (100%)
    pallas_call x1, Pallas kernels, per_device(): pl.pallas_call(functools.partial(kernel, nb, ns), out_shape=jax.ShapeDtyp...  51.7 us
    pallas_call x1, Pallas kernels, per_device(): pl.pallas_call(functools.partial(hand_back, parts), out_shape=jax.ShapeDt...  17 us

profile of v2, /device:TPU:0, one launch (start us, length us, event | category | flops | bytes accessed | tf_op | source)
XLA Modules:
  0.0 68.7 jit_solution(7446837431519315918)
XLA Ops:
  0.0 51.7 %shard_map.73.source = f32[16,64,128]{2,1,0:T(8,128)} custom-call(s32[8,128]{1,0:T(8,128)} %bitcast.6, s32[8,128]{1,0:T(8,128)} %bitcast.7, f32[16,64,128]{2,1,0:T(8,128)} %p_ref.1, f32[16,64,128]{2,1,0:T(8,128)} %r_ref.1, f32[16,64,128]{2,1,0:T(8,128)} %k_ref.1, f32[128,128]{1,0:T(8,128)} %bitcast.4, f32[128,128]{1,0:T(8,128)} %bitcast.5), custom_call_target="tpu_custom_call" | custom-call | tf_op jit(solution)/shard_map/pallas_call | solution.py:414
  51.7 17.0 %shard_map.74 = f32[16,64,128]{2,1,0:T(8,128)} custom-call(f32[16,64,128]{2,1,0:T(8,128)} %shard_map.73.source), custom_call_target="tpu_custom_call" | custom-call | tf_op jit(solution)/shard_map/pallas_call | solution.py:470

commit v3 on v2

--- a/solution.py
+++ b/solution.py
@@ -180,12 +180,26 @@
             ref[*lead, x + 1, PAD - 1 : PAD] = source[*lead, 0, x : x + 1]
             ref[*lead, x + 1, PAD + cy : PAD + cy + 1] = source[*lead, 1, x : x + 1]
 
-    def planes(body):
+    def planes(body, unroll):
         def step(x, carry):
             body(x)
             return carry
 
-        lax.fori_loop(0, cx, step, 0, unroll=4)
+        lax.fori_loop(1, cx - 1, step, 0, unroll=unroll)
+
+    def x_edges(body):
+        body(0, 0, cy)
+        body(cx - 1, 0, cy)
+
+    def y_edges(body, depth):
+        def both(x):
+            body(x, 0, depth)
+            body(x, cy - depth, depth)
+
+        planes(both, True)
+
+    def interior(body, depth):
+        planes(lambda x: body(x, depth, cy - 2 * depth), 2)
 
     loads[0].wait()
     stage_rows(v, (0,), ysend)
@@ -198,64 +212,92 @@
     start_all(copies_of(0))
     each(nb, onehots)
     loads[4].wait()
-    recv_all(k_copies())
-    place_rows(kyhalo, (), k)
-
-    def coefficients(x):
-        here = k[x + 1, PAD : PAD + cy]
-        west = 0.5 * (here + k[x, PAD : PAD + cy])
-        east = 0.5 * (here + k[x + 2, PAD : PAD + cy])
-        south = 0.5 * (here + k[x + 1, PAD - 1 : PAD - 1 + cy])
-        north = 0.5 * (here + k[x + 1, PAD + 1 : PAD + 1 + cy])
-        lower = 0.5 * (here + jnp.where(first, 0.0, pltpu.roll(here, 1, 1)))
-        upper = 0.5 * (here + jnp.where(last, 0.0, pltpu.roll(here, nz - 1, 1)))
+
+    def coefficients(x, y, ny):
+        own = slice(PAD + y, PAD + y + ny)
+        at = slice(y, y + ny)
+        here = k[x + 1, own]
+        west = 0.5 * (here + k[x, own])
+        east = 0.5 * (here + k[x + 2, own])
+        south = 0.5 * (here + k[x + 1, PAD + y - 1 : PAD + y - 1 + ny])
+        north = 0.5 * (here + k[x + 1, PAD + y + 1 : PAD + y + 1 + ny])
+        lower = 0.5 * (here + jnp.where(first[:ny], 0.0, pltpu.roll(here, 1, 1)))
+        upper = 0.5 * (here + jnp.where(last[:ny], 0.0, pltpu.roll(here, nz - 1, 1)))
         total = west + east + south + north + lower + upper
-        fw[x] = west
-        fw[x + 1] = east
-        fs[x] = south
-        fn[x] = north
-        fl[x] = jnp.where(first, 0.0, lower)
-        fu[x] = jnp.where(last, 0.0, upper)
-        diag[x] = total
-        dinv[x] = DAMPING / total
-
-    planes(coefficients)
-
-    def around(stage, x):
-        here = v[stage, x + 1, PAD : PAD + cy]
-        total = rhs[x] + fw[x] * v[stage, x, PAD : PAD + cy] + fw[x + 1] * v[stage, x + 2, PAD : PAD + cy]
-        total = total + fs[x] * v[stage, x + 1, PAD - 1 : PAD - 1 + cy]
-        total = total + fn[x] * v[stage, x + 1, PAD + 1 : PAD + 1 + cy]
-        total = total + fl[x] * pltpu.roll(here, 1, 1) + fu[x] * pltpu.roll(here, nz - 1, 1)
+        fw[x, at] = west
+        fw[x + 1, at] = east
+        fs[x, at] = south
+        fn[x, at] = north
+        fl[x, at] = jnp.where(first[:ny], 0.0, lower)
+        fu[x, at] = jnp.where(last[:ny], 0.0, upper)
+        diag[x, at] = total
+        dinv[x, at] = DAMPING / total
+
+    def around(stage, x, y, ny):
+        own = slice(PAD + y, PAD + y + ny)
+        at = slice(y, y + ny)
+        here = v[stage, x + 1, own]
+        total = rhs[x, at] + fw[x, at] * v[stage, x, own] + fw[x + 1, at] * v[stage, x + 2, own]
+        total = total + fs[x, at] * v[stage, x + 1, PAD + y - 1 : PAD + y - 1 + ny]
+        total = total + fn[x, at] * v[stage, x + 1, PAD + y + 1 : PAD + y + 1 + ny]
+        total = total + fl[x, at] * pltpu.roll(here, 1, 1) + fu[x, at] * pltpu.roll(here, nz - 1, 1)
         return total, here
+
+    def smooth(stage):
+        def body(x, y, ny):
+            total, here = around(stage, x, y, ny)
+            at = slice(y, y + ny)
+            v[stage + 1, x + 1, PAD + y : PAD + y + ny] = (1 - DAMPING) * here + dinv[x, at] * total
+
+        return body
+
+    def residual(x, y, ny):
+        total, here = around(SWEEPS, x, y, ny)
+        start = x * cy + y
+        if not isinstance(x, int):
+            start = pl.multiple_of(start, 2 * PAD)
+        rp[pl.ds(start, ny), :] = pieces_of(total - diag[x, y : y + ny] * here)
+
+    def finish(x, y, ny):
+        at = slice(y, y + ny)
+        total, here = around(2 * SWEEPS, x, y, ny)
+        out_ref[x, at] = (1 - DAMPING) * here + dinv[x, at] * total
 
     def halo_in(stage):
         recv_all(copies_of(stage))
         place_rows(yhalo, (stage,), v)
 
-    def halo_out(stage):
+    def edges_out(body, stage):
+        copies = copies_of(stage)
+        x_edges(body)
+        for there, copy in zip(to[:2], copies[:2]):
+            pl.when(there)(copy.start)
+        y_edges(body, PAD)
         stage_rows(v, (stage,), ysend)
-        start_all(copies_of(stage))
-
-    def smooth(stage):
-        def body(x):
-            total, here = around(stage, x)
-            v[stage + 1, x + 1, PAD : PAD + cy] = (1 - DAMPING) * here + dinv[x] * total
-
-        planes(body)
-
-    for stage in range(SWEEPS):
+        for there, copy in zip(to[2:], copies[2:]):
+            pl.when(there)(copy.start)
+
+    def sweep_on(stage):
+        body = smooth(stage)
+        interior(body, PAD)
         halo_in(stage)
-        smooth(stage)
-        halo_out(stage + 1)
-
+        edges_out(body, stage + 1)
+
+    interior(coefficients, PAD)
+    interior(smooth(0), PAD)
+    recv_all(k_copies())
+    place_rows(kyhalo, (), k)
+    x_edges(coefficients)
+    y_edges(coefficients, PAD)
+    halo_in(0)
+    edges_out(smooth(0), 1)
+    for stage in range(1, SWEEPS):
+        sweep_on(stage)
+
+    interior(residual, 2 * PAD)
     halo_in(SWEEPS)
-
-    def residual(x):
-        total, here = around(SWEEPS, x)
-        rp[pl.ds(pl.multiple_of(x * cy, cy), cy), :] = pieces_of(total - diag[x] * here)
-
-    planes(residual)
+    x_edges(residual)
+    y_edges(residual, 2 * PAD)
 
     def pair_copy(source, target, q, sends, recvs):
         return pltpu.make_async_remote_copy(
@@ -275,7 +317,7 @@
     def rs_copy(q):
         return far_copy(part.at[q], arrived.at[q], q, q, rs_send, rs_recv)
 
-    group = 4 if half % 4 == 0 else 1
+    group = 2 if half % 2 == 0 else 1
 
     def scatter(first_slot):
         hot = spread[pl.ds(first_slot, group)].reshape(group * cr, rows)
@@ -330,8 +372,9 @@
     each(half - 1, lambda q: ag_copy(q).start())
     cx_copy(half - 1).start()
 
-    def hand_over(q):
-        ag_copy(half - 2 - q).wait_recv()
+    def hand_over(i):
+        q = half - 2 - i
+        ag_copy(i).wait_recv()
         cx_copy(q).start()
 
     each(half - 1, hand_over)
@@ -342,34 +385,32 @@
         product = joined(jnp.dot(hot, values, preferred_element_type=jnp.float32), nz)
         acc[...] = product if fresh else acc[...] + product
 
-    if half == group:
-        collect(0, True)
-    else:
-        acc[...] = jnp.zeros((rows, nz), jnp.float32)
-        each(half // group, lambda g: collect(g * group, False))
-    each(half, lambda q: cx_copy(q).wait_recv())
-    each(half // group, lambda g: collect(half + g * group, False))
-
-    def corrected(x):
-        v[SWEEPS + 1, x + 1, PAD : PAD + cy] = (
-            v[SWEEPS, x + 1, PAD : PAD + cy] + acc[pl.ds(pl.multiple_of(x * cy, cy), cy), :]
-        )
-
-    planes(corrected)
-    halo_out(SWEEPS + 1)
-
+    collect(half - group, True)
+    each(half // group - 1, lambda g: collect(half - (g + 2) * group, False))
+
+    def collect_crossed(g):
+        low = half - (g + 1) * group
+        each(group, lambda i: cx_copy(low + group - 1 - i).wait_recv())
+        collect(half + low, False)
+
+    each(half // group, collect_crossed)
+
+    def corrected(x, y, ny):
+        start = x * cy + y
+        if not isinstance(x, int):
+            start = pl.multiple_of(start, PAD)
+        own = slice(PAD + y, PAD + y + ny)
+        v[SWEEPS + 1, x + 1, own] = v[SWEEPS, x + 1, own] + acc[pl.ds(start, ny), :]
+
+    edges_out(corrected, SWEEPS + 1)
+    interior(corrected, PAD)
     for stage in range(SWEEPS + 1, 2 * SWEEPS):
-        halo_in(stage)
-        smooth(stage)
-        halo_out(stage + 1)
-
+        sweep_on(stage)
+
+    interior(finish, PAD)
     halo_in(2 * SWEEPS)
-
-    def finish(x):
-        total, here = around(2 * SWEEPS, x)
-        out_ref[x] = (1 - DAMPING) * here + dinv[x] * total
-
-    planes(finish)
+    x_edges(finish)
+    y_edges(finish, PAD)
     result = pltpu.make_async_copy(out_ref, out_hbm, out_sem)
     result.start()
 
@@ -383,18 +424,25 @@
     result.wait()
 
 
-def hand_back(parts, source, target, sems):
+def hand_back(parts, source, target, held, load_sems, store_sems):
     size = source.shape[0] // parts
-    copies = [
-        pltpu.make_async_copy(
-            source.at[pl.ds(i * size, size)], target.at[pl.ds(i * size, size)], sems.at[i]
-        )
-        for i in range(parts)
-    ]
-    for copy in copies:
-        copy.start()
-    for copy in copies:
-        copy.wait()
+
+    def copies(first, second, sems):
+        return [
+            pltpu.make_async_copy(
+                first.at[pl.ds(i * size, size)], second.at[pl.ds(i * size, size)], sems.at[i]
+            )
+            for i in range(parts)
+        ]
+
+    loads, stores = copies(source, held, load_sems), copies(held, target, store_sems)
+    for load in loads:
+        load.start()
+    for load, store in zip(loads, stores):
+        load.wait()
+        store.start()
+    for store in stores:
+        store.wait()
 
 
 def per_device(nb, ns, pressure, rhs, kappa, owner, coarse_row, coarse_leak, coarse_link):
@@ -472,7 +520,7 @@
         out_shape=jax.ShapeDtypeStruct(block, f32),
         in_specs=[hbm],
         out_specs=hbm,
-        scratch_shapes=[dma((parts,))],
+        scratch_shapes=[pltpu.VMEM(block, f32), dma((parts,)), dma((parts,))],
         compiler_params=pltpu.CompilerParams(vmem_limit_bytes=60 * 2**20),
     )(result)
 

time: 68.9 us -> 49.3 us (0.72)
  Pallas kernels: 68.7 us -> 49.2 us
    pallas_call x1, Pallas kernels: 17 us -> 1.82 us  [per_device(): pl.pallas_call(functools.partial(hand_back, parts), out_shape=jax.ShapeDt...]
    pallas_call x1, Pallas kernels: 51.7 us -> 47.4 us  [per_device(): pl.pallas_call(functools.partial(kernel, nb, ns), out_shape=jax.ShapeDtyp...]
where the time goes in v3:
time: 49.3 us; the launch traced here: 49.2 us
  Pallas kernels  49.2 us (100%)
    pallas_call x1, Pallas kernels, per_device(): pl.pallas_call(functools.partial(kernel, nb, ns), out_shape=jax.ShapeDtyp...  47.4 us
    pallas_call x1, Pallas kernels, per_device(): pl.pallas_call(functools.partial(hand_back, parts), out_shape=jax.ShapeDt...  1.82 us

profile of v3, /device:TPU:0, one launch (start us, length us, event | category | flops | bytes accessed | tf_op | source)
XLA Modules:
  0.0 49.2 jit_solution(7633186929998422917)
XLA Ops:
  0.0 47.4 %shard_map.73.source = f32[16,64,128]{2,1,0:T(8,128)} custom-call(s32[8,128]{1,0:T(8,128)} %bitcast.6, s32[8,128]{1,0:T(8,128)} %bitcast.7, f32[16,64,128]{2,1,0:T(8,128)} %p_ref.1, f32[16,64,128]{2,1,0:T(8,128)} %r_ref.1, f32[16,64,128]{2,1,0:T(8,128)} %k_ref.1, f32[128,128]{1,0:T(8,128)} %bitcast.4, f32[128,128]{1,0:T(8,128)} %bitcast.5), custom_call_target="tpu_custom_call" | custom-call | tf_op jit(solution)/shard_map/pallas_call | solution.py:462
  47.4 1.8 %shard_map.74 = f32[16,64,128]{2,1,0:T(8,128)} custom-call(f32[16,64,128]{2,1,0:T(8,128)} %shard_map.73.source), custom_call_target="tpu_custom_call" | custom-call | tf_op jit(solution)/shard_map/pallas_call | solution.py:518

commit v4 on v3

--- a/solution.py
+++ b/solution.py
@@ -44,11 +44,11 @@
 
 
 def kernel(
-    nb, ns, owner_ref, row_ref, p_ref, r_ref, k_ref, leak_hbm, link_hbm, out_hbm,
-    key_ref, row_key, leak_ref, link_ref, out_ref, v, k, rhs, fw, fs, fn, fl, fu, diag, dinv, ysend, yhalo, kysend, kyhalo,
+    nb, ns, owner_ref, row_ref, p_ref, r_ref, k_ref, leak_hbm, link_hbm, out_ref,
+    key_ref, row_key, leak_ref, link_ref, v, k, rhs, fw, fs, fn, fl, fu, diag, dinv, ysend, yhalo, kysend, kyhalo,
     spread, gather, keycol, rp, part, crossed, arrived, corr, acc,
     load_sem, send_sem, recv_sem, ksend_sem, krecv_sem,
-    rs_send, rs_recv, ag_send, ag_recv, px_send, px_recv, cx_send, cx_recv, out_sem,
+    rs_send, rs_recv, ag_send, ag_recv, px_send, px_recv, cx_send, cx_recv,
 ):
     cx, cy, nz = out_ref.shape
     cr = leak_ref.shape[0]
@@ -109,24 +109,27 @@
     place, side = b // 2, lax.rem(b, 2)
     other = 1 - side
     lanes = key_ref.shape[1]
-    loads[2].wait()
-    loads[3].wait()
-    key_ref[...] = key_ref[...] * cr + row_key[...]
-
     def pair_at(q):
         return lax.rem(place + q + 1, half) * 2
 
-    for a in range(key_ref.shape[0]):
-        wide = jnp.broadcast_to(key_ref[a : a + 1, :], (lanes, lanes)).astype(jnp.float32)
-        keycol[a * lanes : (a + 1) * lanes, :] = wide.T.astype(jnp.int32)
-
-    def onehots(j):
-        base = (pair_at(j) + jnp.where(j < half, side, other)) * cr
-        down = lax.broadcasted_iota(jnp.int32, (cr, lanes), 0) + base
-        across = lax.broadcasted_iota(jnp.int32, (lanes, cr), 1) + base
+
+    def base_of(j):
+        return (pair_at(j) + jnp.where(j < half, side, other)) * cr
+
+    def spread_onehot(j):
+        down = lax.broadcasted_iota(jnp.int32, (cr, lanes), 0) + base_of(j)
         for a in range(key_ref.shape[0]):
             hit = jnp.broadcast_to(key_ref[a : a + 1, :], (cr, lanes)) == down
             spread[j, :, a * lanes : (a + 1) * lanes] = jnp.where(hit, 1.0, 0.0).astype(jnp.bfloat16)
+
+    def key_columns():
+        for a in range(key_ref.shape[0]):
+            wide = jnp.broadcast_to(key_ref[a : a + 1, :], (lanes, lanes)).astype(jnp.float32)
+            keycol[a * lanes : (a + 1) * lanes, :] = wide.T.astype(jnp.int32)
+
+    def gather_onehot(j):
+        across = lax.broadcasted_iota(jnp.int32, (lanes, cr), 1) + base_of(j)
+        for a in range(key_ref.shape[0]):
             hit = keycol[a * lanes : (a + 1) * lanes, :cr] == across
             gather[j, a * lanes : (a + 1) * lanes, :] = jnp.where(hit, 1.0, 0.0).astype(jnp.bfloat16)
 
@@ -210,7 +213,6 @@
 
     start_all(k_copies())
     start_all(copies_of(0))
-    each(nb, onehots)
     loads[4].wait()
 
     def coefficients(x, y, ny):
@@ -291,10 +293,15 @@
     y_edges(coefficients, PAD)
     halo_in(0)
     edges_out(smooth(0), 1)
+    loads[2].wait()
+    loads[3].wait()
+    key_ref[...] = key_ref[...] * cr + row_key[...]
+    each(nb, spread_onehot)
     for stage in range(1, SWEEPS):
         sweep_on(stage)
 
     interior(residual, 2 * PAD)
+    key_columns()
     halo_in(SWEEPS)
     x_edges(residual)
     y_edges(residual, 2 * PAD)
@@ -345,6 +352,7 @@
         rs_copy(q).start()
 
     each(half - 1, pass_on)
+    each(half, gather_onehot)
     px_copy(half - 1).wait_recv()
     coarse = part[half - 1] + crossed[half - 1]
     if half <= 8:
@@ -371,6 +379,7 @@
 
     each(half - 1, lambda q: ag_copy(q).start())
     cx_copy(half - 1).start()
+    each(half, lambda q: gather_onehot(half + q))
 
     def hand_over(i):
         q = half - 2 - i
@@ -411,8 +420,6 @@
     halo_in(2 * SWEEPS)
     x_edges(finish)
     y_edges(finish, PAD)
-    result = pltpu.make_async_copy(out_ref, out_hbm, out_sem)
-    result.start()
 
     send_all(k_copies())
     for stage in range(2 * SWEEPS + 1):
@@ -421,28 +428,20 @@
     each(half, lambda q: cx_copy(q).wait_send())
     each(half - 1, lambda q: rs_copy(q).wait_send())
     each(half - 1, lambda q: ag_copy(q).wait_send())
-    result.wait()
-
-
-def hand_back(parts, source, target, held, load_sems, store_sems):
+
+
+def hand_back(parts, source, target, sems):
     size = source.shape[0] // parts
-
-    def copies(first, second, sems):
-        return [
-            pltpu.make_async_copy(
-                first.at[pl.ds(i * size, size)], second.at[pl.ds(i * size, size)], sems.at[i]
-            )
-            for i in range(parts)
-        ]
-
-    loads, stores = copies(source, held, load_sems), copies(held, target, store_sems)
-    for load in loads:
-        load.start()
-    for load, store in zip(loads, stores):
-        load.wait()
-        store.start()
-    for store in stores:
-        store.wait()
+    copies = [
+        pltpu.make_async_copy(
+            source.at[pl.ds(i * size, size)], target.at[pl.ds(i * size, size)], sems.at[i]
+        )
+        for i in range(parts)
+    ]
+    for copy in copies:
+        copy.start()
+    for copy in copies:
+        copy.wait()
 
 
 def per_device(nb, ns, pressure, rhs, kappa, owner, coarse_row, coarse_leak, coarse_link):
@@ -457,19 +456,18 @@
     block = (cx, cy, nz)
     padded = (cx + 2, cy + 2 * PAD, nz)
     vmem = pl.BlockSpec(memory_space=pltpu.VMEM)
-    hbm = pl.BlockSpec(memory_space=pl.ANY)
+    hbm = pl.BlockSpec(memory_space=pltpu.HBM)
     dma = pltpu.SemaphoreType.DMA
     result = pl.pallas_call(
         functools.partial(kernel, nb, ns),
-        out_shape=jax.ShapeDtypeStruct(block, f32),
+        out_shape=pltpu.VMEM(block, f32),
         in_specs=[hbm] * 7,
-        out_specs=hbm,
+        out_specs=vmem,
         scratch_shapes=[
             pltpu.VMEM(keys, jnp.int32),
             pltpu.VMEM(keys, jnp.int32),
             pltpu.VMEM((cr, nz), f32),
             pltpu.VMEM((cr, nz), f32),
-            pltpu.VMEM(block, f32),
             pltpu.VMEM((stages,) + padded, f32),
             pltpu.VMEM(padded, f32),
             pltpu.VMEM(block, f32),
@@ -506,10 +504,9 @@
             dma((nb // 2,)),
             dma((nb // 2,)),
             dma((nb // 2,)),
-            dma,
         ],
         compiler_params=pltpu.CompilerParams(
-            collective_id=0, has_side_effects=True, vmem_limit_bytes=60 * 2**20
+            collective_id=0, has_side_effects=True, vmem_limit_bytes=58 * 2**20
         ),
     )(
         owner.reshape(keys), coarse_row.reshape(keys), pressure, rhs, kappa,
@@ -518,10 +515,10 @@
     return pl.pallas_call(
         functools.partial(hand_back, parts),
         out_shape=jax.ShapeDtypeStruct(block, f32),
-        in_specs=[hbm],
+        in_specs=[vmem],
         out_specs=hbm,
-        scratch_shapes=[pltpu.VMEM(block, f32), dma((parts,)), dma((parts,))],
-        compiler_params=pltpu.CompilerParams(vmem_limit_bytes=60 * 2**20),
+        scratch_shapes=[dma((parts,))],
+        compiler_params=pltpu.CompilerParams(vmem_limit_bytes=16 * 2**20),
     )(result)
 
 

time: 49.3 us -> 48.2 us (0.978)
  Pallas kernels: 49.2 us -> 48 us
    pallas_call x1, Pallas kernels: 1.82 us -> 0.82 us  [per_device(): pl.pallas_call(functools.partial(hand_back, parts), out_shape=jax.ShapeDt...]
where the time goes in v4:
time: 48.2 us; the launch traced here: 48.1 us
  Pallas kernels  48 us (100%)
    pallas_call x1, Pallas kernels, per_device(): pl.pallas_call(functools.partial(kernel, nb, ns), out_shape=pltpu.VMEM(bl...  47.2 us

profile of v4, /device:TPU:0, one launch (start us, length us, event | category | flops | bytes accessed | tf_op | source)
XLA Modules:
  0.0 48.1 jit_solution(10979017294636609195)
XLA Ops:
  0.0 47.2 %shard_map.73.source = f32[16,64,128]{2,1,0:T(8,128)S(1)} custom-call(s32[8,128]{1,0:T(8,128)} %bitcast.6, s32[8,128]{1,0:T(8,128)} %bitcast.7, f32[16,64,128]{2,1,0:T(8,128)} %p_ref.1, f32[16,64,128]{2,1,0:T(8,128)} %r_ref.1, f32[16,64,128]{2,1,0:T(8,128)} %k_ref.1, f32[128,128]{1,0:T(8,128)} %bitcast.4, f32[128,128]{1,0:T(8,128)} %bitcast.5), custom_call_target="tpu_custom_call" | custom-call | tf_op jit(solution)/shard_map/pallas_call | solution.py:461
  47.2 0.8 %shard_map.74 = f32[16,64,128]{2,1,0:T(8,128)} custom-call(f32[16,64,128]{2,1,0:T(8,128)S(1)} %shard_map.73.source), custom_call_target="tpu_custom_call" | custom-call | tf_op jit(solution)/shard_map/pallas_call | solution.py:515

commit v5 on v4

--- a/solution.py
+++ b/solution.py
@@ -106,6 +106,7 @@
                 yhalo[stage, edge] = jnp.zeros((cx, nz), jnp.float32)
 
     half = nb // 2
+    cuts = px_send.shape[0] // half
     place, side = b // 2, lax.rem(b, 2)
     other = 1 - side
     lanes = key_ref.shape[1]
@@ -306,23 +307,27 @@
     x_edges(residual)
     y_edges(residual, 2 * PAD)
 
-    def pair_copy(source, target, q, sends, recvs):
+    def piece(ref, first_slot, n):
+        size = cr // cuts
+        return ref.at[first_slot + n // cuts, pl.ds((n % cuts) * size, size)]
+
+    def pair_copy(source, target, n, sends, recvs):
         return pltpu.make_async_remote_copy(
-            src_ref=source, dst_ref=target, send_sem=sends.at[q], recv_sem=recvs.at[q],
+            src_ref=source, dst_ref=target, send_sem=sends.at[n], recv_sem=recvs.at[n],
             device_id={"bulk": 2 * place + other}, device_id_type=pl.DeviceIdType.MESH,
         )
 
-    def far_copy(source, target, q, slot, sends, recvs):
+    def far_copy(source, target, q, n, sends, recvs):
         return pltpu.make_async_remote_copy(
-            src_ref=source, dst_ref=target, send_sem=sends.at[slot], recv_sem=recvs.at[slot],
+            src_ref=source, dst_ref=target, send_sem=sends.at[n], recv_sem=recvs.at[n],
             device_id={"bulk": pair_at(q) + side}, device_id_type=pl.DeviceIdType.MESH,
         )
 
-    def px_copy(q):
-        return pair_copy(part.at[half + q], crossed.at[q], q, px_send, px_recv)
-
-    def rs_copy(q):
-        return far_copy(part.at[q], arrived.at[q], q, q, rs_send, rs_recv)
+    def px_copy(n):
+        return pair_copy(piece(part, half, n), piece(crossed, 0, n), n, px_send, px_recv)
+
+    def rs_copy(n):
+        return far_copy(piece(part, 0, n), piece(arrived, 0, n), n // cuts, n, rs_send, rs_recv)
 
     group = 2 if half % 2 == 0 else 1
 
@@ -333,7 +338,7 @@
 
     def scatter_across(g):
         scatter(half + g * group)
-        each(group, lambda i: px_copy(g * group + i).start())
+        each(group * cuts, lambda i: px_copy(g * group * cuts + i).start())
 
     each(half // group, scatter_across)
     each(half // group, lambda g: scatter(g * group))
@@ -346,21 +351,22 @@
     cinv = DAMPING / (leak_ref[...] + link + below)
     above = jnp.where(zc == nz - 1, 0.0, link)
 
-    def pass_on(q):
-        px_copy(q).wait_recv()
-        part[q] = part[q] + crossed[q]
-        rs_copy(q).start()
-
-    each(half - 1, pass_on)
+    def pass_on(n):
+        px_copy(n).wait_recv()
+        rows_of = pl.ds((n % cuts) * (cr // cuts), cr // cuts)
+        part[n // cuts, rows_of] = part[n // cuts, rows_of] + crossed[n // cuts, rows_of]
+        rs_copy(n).start()
+
+    own = (half - 1) * cuts
+    each(own, pass_on)
     each(half, gather_onehot)
-    px_copy(half - 1).wait_recv()
+    each(cuts, lambda h: px_copy(own + h).wait_recv())
     coarse = part[half - 1] + crossed[half - 1]
+    each(own, lambda n: rs_copy(n).wait_recv())
     if half <= 8:
         for q in range(half - 1):
-            rs_copy(q).wait_recv()
             coarse = coarse + arrived[q]
     else:
-        each(half - 1, lambda q: rs_copy(q).wait_recv())
         coarse = lax.fori_loop(0, half - 1, lambda q, total: total + arrived[q], coarse)
 
     u = cinv * coarse
@@ -370,23 +376,23 @@
         )
     corr[half - 1] = u
 
-    def ag_copy(q):
-        slot = half - 2 - q
-        return far_copy(corr.at[half - 1], corr.at[slot], q, slot, ag_send, ag_recv)
-
-    def cx_copy(q):
-        return pair_copy(corr.at[q], corr.at[half + q], q, cx_send, cx_recv)
-
-    each(half - 1, lambda q: ag_copy(q).start())
-    cx_copy(half - 1).start()
+    def ag_copy(n):
+        q, h = n // cuts, (n % cuts)
+        slot = (half - 2 - q) * cuts + h
+        return far_copy(piece(corr, 0, own + h), piece(corr, 0, slot), q, slot, ag_send, ag_recv)
+
+    def cx_copy(n):
+        return pair_copy(piece(corr, 0, n), piece(corr, half, n), n, cx_send, cx_recv)
+
+    each(own, lambda n: ag_copy(n).start())
+    each(cuts, lambda h: cx_copy(own + h).start())
     each(half, lambda q: gather_onehot(half + q))
 
-    def hand_over(i):
-        q = half - 2 - i
-        ag_copy(i).wait_recv()
-        cx_copy(q).start()
-
-    each(half - 1, hand_over)
+    def hand_over(n):
+        ag_copy(n).wait_recv()
+        cx_copy((half - 2 - n // cuts) * cuts + (n % cuts)).start()
+
+    each(own, hand_over)
 
     def collect(first_slot, fresh):
         values = pieces_of(corr[pl.ds(first_slot, group)].reshape(group * cr, nz))
@@ -399,7 +405,7 @@
 
     def collect_crossed(g):
         low = half - (g + 1) * group
-        each(group, lambda i: cx_copy(low + group - 1 - i).wait_recv())
+        each(group * cuts, lambda i: cx_copy(low * cuts + i).wait_recv())
         collect(half + low, False)
 
     each(half // group, collect_crossed)
@@ -424,10 +430,10 @@
     send_all(k_copies())
     for stage in range(2 * SWEEPS + 1):
         send_all(copies_of(stage))
-    each(half, lambda q: px_copy(q).wait_send())
-    each(half, lambda q: cx_copy(q).wait_send())
-    each(half - 1, lambda q: rs_copy(q).wait_send())
-    each(half - 1, lambda q: ag_copy(q).wait_send())
+    each(half * cuts, lambda n: px_copy(n).wait_send())
+    each(half * cuts, lambda n: cx_copy(n).wait_send())
+    each(own, lambda n: rs_copy(n).wait_send())
+    each(own, lambda n: ag_copy(n).wait_send())
 
 
 def hand_back(parts, source, target, sems):
@@ -449,6 +455,7 @@
     cr = coarse_leak.shape[1]
     rows = cx * cy
     lanes = 128
+    cuts = 2 if cr % 16 == 0 else 1
     keys = (rows // lanes, lanes)
     parts = 4 if cx % 4 == 0 else 1
     stages = 2 * SWEEPS + 1
@@ -496,14 +503,14 @@
             dma((stages, 4)),
             dma((4,)),
             dma((4,)),
-            dma((nb // 2,)),
-            dma((nb // 2,)),
-            dma((nb // 2,)),
-            dma((nb // 2,)),
-            dma((nb // 2,)),
-            dma((nb // 2,)),
-            dma((nb // 2,)),
-            dma((nb // 2,)),
+            dma((nb // 2 * cuts,)),
+            dma((nb // 2 * cuts,)),
+            dma((nb // 2 * cuts,)),
+            dma((nb // 2 * cuts,)),
+            dma((nb // 2 * cuts,)),
+            dma((nb // 2 * cuts,)),
+            dma((nb // 2 * cuts,)),
+            dma((nb // 2 * cuts,)),
         ],
         compiler_params=pltpu.CompilerParams(
             collective_id=0, has_side_effects=True, vmem_limit_bytes=58 * 2**20

time: 48.2 us -> 47.5 us (0.985)
  Pallas kernels: 48 us -> 47.4 us
    pallas_call x1, Pallas kernels: 47.2 us -> 46.5 us  [per_device(): pl.pallas_call(functools.partial(kernel, nb, ns), out_shape=pltpu.VMEM(bl...]
where the time goes in v5:
time: 47.5 us; the launch traced here: 47.4 us
  Pallas kernels  47.4 us (100%)
    pallas_call x1, Pallas kernels, per_device(): pl.pallas_call(functools.partial(kernel, nb, ns), out_shape=pltpu.VMEM(bl...  46.5 us

profile of v5, /device:TPU:0, one launch (start us, length us, event | category | flops | bytes accessed | tf_op | source)
XLA Modules:
  0.0 47.4 jit_solution(4877533177709502475)
XLA Ops:
  0.0 46.5 %shard_map.73.source = f32[16,64,128]{2,1,0:T(8,128)S(1)} custom-call(s32[8,128]{1,0:T(8,128)} %bitcast.6, s32[8,128]{1,0:T(8,128)} %bitcast.7, f32[16,64,128]{2,1,0:T(8,128)} %p_ref.1, f32[16,64,128]{2,1,0:T(8,128)} %r_ref.1, f32[16,64,128]{2,1,0:T(8,128)} %k_ref.1, f32[128,128]{1,0:T(8,128)} %bitcast.4, f32[128,128]{1,0:T(8,128)} %bitcast.5), custom_call_target="tpu_custom_call" | custom-call | tf_op jit(solution)/shard_map/pallas_call | solution.py:468
  46.5 0.8 %shard_map.74 = f32[16,64,128]{2,1,0:T(8,128)} custom-call(f32[16,64,128]{2,1,0:T(8,128)S(1)} %shard_map.73.source), custom_call_target="tpu_custom_call" | custom-call | tf_op jit(solution)/shard_map/pallas_call | solution.py:522

commit v6 on v5

--- a/solution.py
+++ b/solution.py
@@ -384,8 +384,8 @@
     def cx_copy(n):
         return pair_copy(piece(corr, 0, n), piece(corr, half, n), n, cx_send, cx_recv)
 
+    each(cuts, lambda h: cx_copy(own + h).start())
     each(own, lambda n: ag_copy(n).start())
-    each(cuts, lambda h: cx_copy(own + h).start())
     each(half, lambda q: gather_onehot(half + q))
 
     def hand_over(n):
@@ -394,21 +394,24 @@
 
     each(own, hand_over)
 
-    def collect(first_slot, fresh):
+    def collect(first_slot, fresh, spans=((0, rows),), between=()):
         values = pieces_of(corr[pl.ds(first_slot, group)].reshape(group * cr, nz))
-        hot = jnp.concatenate([gather[first_slot + i] for i in range(group)], axis=1)
-        product = joined(jnp.dot(hot, values, preferred_element_type=jnp.float32), nz)
-        acc[...] = product if fresh else acc[...] + product
+        for index, (low, high) in enumerate(spans):
+            hot = jnp.concatenate([gather[first_slot + i, low:high] for i in range(group)], axis=1)
+            product = joined(jnp.dot(hot, values, preferred_element_type=jnp.float32), nz)
+            acc[low:high] = product if fresh else acc[low:high] + product
+            if index < len(between):
+                between[index]()
 
     collect(half - group, True)
     each(half // group - 1, lambda g: collect(half - (g + 2) * group, False))
 
-    def collect_crossed(g):
+    def collect_crossed(g, *order):
         low = half - (g + 1) * group
         each(group * cuts, lambda i: cx_copy(low * cuts + i).wait_recv())
-        collect(half + low, False)
-
-    each(half // group, collect_crossed)
+        collect(half + low, False, *order)
+
+    each(half // group - 1, collect_crossed)
 
     def corrected(x, y, ny):
         start = x * cy + y
@@ -417,7 +420,20 @@
         own = slice(PAD + y, PAD + y + ny)
         v[SWEEPS + 1, x + 1, own] = v[SWEEPS, x + 1, own] + acc[pl.ds(start, ny), :]
 
-    edges_out(corrected, SWEEPS + 1)
+    copies = copies_of(SWEEPS + 1)
+
+    def send_x():
+        x_edges(corrected)
+        for there, copy in zip(to[:2], copies[:2]):
+            pl.when(there)(copy.start)
+
+    collect_crossed(
+        half // group - 1, ((0, cy), (rows - cy, rows), (cy, rows - cy)), (lambda: None, send_x)
+    )
+    y_edges(corrected, PAD)
+    stage_rows(v, (SWEEPS + 1,), ysend)
+    for there, copy in zip(to[2:], copies[2:]):
+        pl.when(there)(copy.start)
     interior(corrected, PAD)
     for stage in range(SWEEPS + 1, 2 * SWEEPS):
         sweep_on(stage)

time: 47.5 us -> 47.3 us (level)
  no operation moved by 1% of the time
where the time goes in v6:
time: 47.3 us; the launch traced here: 47.2 us
  Pallas kernels  47.1 us (100%)
    pallas_call x1, Pallas kernels, per_device(): pl.pallas_call(functools.partial(kernel, nb, ns), out_shape=pltpu.VMEM(bl...  46.3 us

profile of v6, /device:TPU:0, one launch (start us, length us, event | category | flops | bytes accessed | tf_op | source)
XLA Modules:
  0.0 47.2 jit_solution(1439381026440496838)
XLA Ops:
  0.0 46.3 %shard_map.73.source = f32[16,64,128]{2,1,0:T(8,128)S(1)} custom-call(s32[8,128]{1,0:T(8,128)} %bitcast.6, s32[8,128]{1,0:T(8,128)} %bitcast.7, f32[16,64,128]{2,1,0:T(8,128)} %p_ref.1, f32[16,64,128]{2,1,0:T(8,128)} %r_ref.1, f32[16,64,128]{2,1,0:T(8,128)} %k_ref.1, f32[128,128]{1,0:T(8,128)} %bitcast.4, f32[128,128]{1,0:T(8,128)} %bitcast.5), custom_call_target="tpu_custom_call" | custom-call | tf_op jit(solution)/shard_map/pallas_call | solution.py:484
  46.3 0.8 %shard_map.74 = f32[16,64,128]{2,1,0:T(8,128)} custom-call(f32[16,64,128]{2,1,0:T(8,128)S(1)} %shard_map.73.source), custom_call_target="tpu_custom_call" | custom-call | tf_op jit(solution)/shard_map/pallas_call | solution.py:538

commit v7 on v6

--- a/solution.py
+++ b/solution.py
@@ -203,7 +203,7 @@
         planes(both, True)
 
     def interior(body, depth):
-        planes(lambda x: body(x, depth, cy - 2 * depth), 2)
+        planes(lambda x: body(x, depth, cy - 2 * depth), 7)
 
     loads[0].wait()
     stage_rows(v, (0,), ysend)

time: 47.3 us -> 47.3 us (level)
  no operation moved by 1% of the time
where the time goes in v7:
time: 47.3 us; the launch traced here: 47.2 us
  Pallas kernels  47.1 us (100%)
    pallas_call x1, Pallas kernels, per_device(): pl.pallas_call(functools.partial(kernel, nb, ns), out_shape=pltpu.VMEM(bl...  46.3 us

profile of v7, /device:TPU:0, one launch (start us, length us, event | category | flops | bytes accessed | tf_op | source)
XLA Modules:
  0.0 47.2 jit_solution(577135253290209418)
XLA Ops:
  0.0 46.3 %shard_map.73.source = f32[16,64,128]{2,1,0:T(8,128)S(1)} custom-call(s32[8,128]{1,0:T(8,128)} %bitcast.6, s32[8,128]{1,0:T(8,128)} %bitcast.7, f32[16,64,128]{2,1,0:T(8,128)} %p_ref.1, f32[16,64,128]{2,1,0:T(8,128)} %r_ref.1, f32[16,64,128]{2,1,0:T(8,128)} %k_ref.1, f32[128,128]{1,0:T(8,128)} %bitcast.4, f32[128,128]{1,0:T(8,128)} %bitcast.5), custom_call_target="tpu_custom_call" | custom-call | tf_op jit(solution)/shard_map/pallas_call | solution.py:484
  46.3 0.8 %shard_map.74 = f32[16,64,128]{2,1,0:T(8,128)} custom-call(f32[16,64,128]{2,1,0:T(8,128)S(1)} %shard_map.73.source), custom_call_target="tpu_custom_call" | custom-call | tf_op jit(solution)/shard_map/pallas_call | solution.py:538
